TPU v7x, 512 devices: a whole 4x8x8 slice. The times are simulated.
512 devices in a mesh: section: 16 (over x, z_lo, core), dp: 32 (over y, z_hi).
Axes of the slice: x: 4, y: 8, z: 8 (z_hi: 4, z_lo: 2; z = z_hi * 2 + z_lo), core: 2. Of those that a mesh axis runs over, the one named last changes fastest.
Arguments:
- inputs: bfloat16 [4, 1024, 2048], P(None, 'dp'), may hold values from -6 to 6
- upstream: bfloat16 [4, 1024, 2048], P(None, 'dp'), may hold values from -6 to 6
- segments: int32 [4, 1024], P(None, 'dp'), may hold values from 0 to 127, never falling along the last dimension, each value on 1 to 16 neighbouring positions
- gains: float32 [16, 2048], P('section'), may hold values from 0.5 to 1.5
- master: float32 [16, 2048, 1024], P('section', 'dp'), may hold values from -0.125 to 0.125
- moment: float32 [16, 2048, 1024], P('section', 'dp'), may hold values from -0.15625 to 0.15625
- second: float32 [16, 2048, 1024], P('section', 'dp'), may hold values from 1e-05 to 0.001
Outputs:
- new_master: float32 [16, 2048, 1024], P('section', 'dp')
- new_moment: float32 [16, 2048, 1024], P('section', 'dp')
- new_second: float32 [16, 2048, 1024], P('section', 'dp')
- replica: bfloat16 [16, 2048, 1024], P('section', 'dp')
Inputs may be any that keep to these rules, and one draw needn't show every extreme that they name: `segments`: segment numbers never fall along a micro-batch; each segment holds 1 to 16 positions, one exactly 16.
All inputs are finite; a program needn't handle non-finite values.
Results may differ from a plain program's by a relative error of at most 0.0065.
Values may be sent and summed in bfloat16 or wider, within the bound.
No kernel may reach another device: no remote copies, remote signals or barrier semaphores. Data moves between devices by JAX's collectives and lax.ppermute only.
A program may use at most 64 MiB of HBM per device.

v0:
```python
import jax
import jax.numpy as jnp
from jax import lax
from jax.sharding import PartitionSpec as P

HEAD = 128


def shifted(block, axis, distance):
    devices = range(lax.axis_size(axis))
    route = [(i - distance, i) for i in devices if i - distance in devices]
    return lax.ppermute(block, axis, route)


def from_behind(block, axis, distance):
    devices = range(lax.axis_size(axis))
    route = [((i - distance) % len(devices), i) for i in devices]
    return lax.ppermute(block, axis, route)


def normed(xf, gain):
    return xf * lax.rsqrt(jnp.mean(xf * xf, axis=-1, keepdims=True) + 1e-05) * gain


def attend(x, h, kv, seg):
    length = x.shape[0]
    width = kv.shape[1] // 2
    kv_heads = width // HEAD
    groups = h.shape[1] // HEAD // kv_heads
    query = h.astype(jnp.float32).reshape(length, kv_heads, groups, HEAD)
    keys = kv[:, :width].astype(jnp.float32).reshape(length, kv_heads, HEAD)
    values = kv[:, width:].astype(jnp.float32).reshape(length, kv_heads, HEAD)
    scores = jnp.einsum("qhgd,khd->hgqk", query, keys) * HEAD ** (-0.5)
    place = jnp.arange(length)
    allowed = (place[:, None] >= place[None, :]) & (seg[:, None] == seg[None, :])
    scores = jnp.where(allowed, scores, -1e30)
    probs = jax.nn.softmax(scores, axis=-1).astype(jnp.bfloat16)
    mixed = jnp.einsum("hgqk,khd->qhgd", probs.astype(jnp.float32), values).reshape(length, -1)
    return (x.astype(jnp.float32) + mixed).astype(jnp.bfloat16)


def forward(x, gain, w, seg):
    h = normed(x.astype(jnp.float32), gain).astype(jnp.bfloat16)
    kv = jnp.dot(h, w, preferred_element_type=jnp.float32).astype(jnp.bfloat16)
    return attend(x, h, kv, seg)


def backward(x, gain, w, seg, dy):
    hf, pull_norm = jax.vjp(lambda v: normed(v, gain), x.astype(jnp.float32))
    hb = hf.astype(jnp.bfloat16)
    kv = jnp.dot(hb, w, preferred_element_type=jnp.float32).astype(jnp.bfloat16)
    _, pull = jax.vjp(lambda a, b, c: attend(a, b, c, seg), x, hb, kv)
    dx_direct, dh_attn, dkv = pull(dy)
    dh = dh_attn.astype(jnp.float32) + lax.dot_general(
        dkv, w, (((1,), (1,)), ((), ())), preferred_element_type=jnp.float32
    )
    dx = (dx_direct.astype(jnp.float32) + pull_norm(dh)[0]).astype(jnp.bfloat16)
    return (dx, hb, dkv)


def send_back(dx):
    return shifted(dx, "section", -1)


def body(inputs, upstream, segments, gains, master, moment, second):
    position = lax.axis_index("section")
    sections = lax.axis_size("section")
    micro = inputs.shape[0]
    length = inputs.shape[1]
    width = inputs.shape[2]
    gain = gains[0]
    whole = lax.all_gather(master[0].astype(jnp.bfloat16), "dp", axis=0, tiled=True)
    kv_cols = whole.shape[1]
    steps = micro + sections - 1

    def fstep(turn, carry):
        incoming, store = carry
        slot_raw = turn - position
        live = (slot_raw >= 0) & (slot_raw < micro)
        slot = jnp.clip(slot_raw, 0, micro - 1)
        first = lax.dynamic_index_in_dim(inputs, slot, 0, keepdims=False)
        seg = lax.dynamic_index_in_dim(segments, slot, 0, keepdims=False)
        xin = jnp.where(position == 0, first, incoming)
        result = lax.cond(live, lambda: forward(xin, gain, whole, seg), lambda: jnp.zeros_like(xin))
        before = lax.dynamic_index_in_dim(store, slot, 0, keepdims=False)
        store = lax.dynamic_update_index_in_dim(store, jnp.where(live, xin, before), slot, 0)
        incoming = shifted(result, "section", 1)
        return (incoming, store)

    start_buf = jnp.zeros((length, width), jnp.bfloat16)
    store0 = jnp.zeros_like(inputs)
    _, store = lax.fori_loop(0, steps, fstep, (start_buf, store0))

    def slot_of(turn):
        slot_raw = turn - (sections - 1 - position)
        live = (slot_raw >= 0) & (slot_raw < micro)
        return (live, jnp.clip(slot_raw, 0, micro - 1))

    def run_back(live, slot, incoming):
        last = lax.dynamic_index_in_dim(upstream, slot, 0, keepdims=False)
        dy = jnp.where(position == sections - 1, last, incoming)
        xin = lax.dynamic_index_in_dim(store, slot, 0, keepdims=False)
        seg = lax.dynamic_index_in_dim(segments, slot, 0, keepdims=False)
        return lax.cond(
            live,
            lambda: backward(xin, gain, whole, seg, dy),
            lambda: (
                jnp.zeros_like(xin),
                jnp.zeros((length, width), jnp.bfloat16),
                jnp.zeros((length, kv_cols), jnp.bfloat16),
            ),
        )

    def bstep(turn, carry):
        incoming, accum = carry
        live, slot = slot_of(turn)
        dx, hb, dkv = run_back(live, slot, incoming)
        accum = accum + lax.dot_general(
            hb, dkv, (((0,), (0,)), ((), ())), preferred_element_type=jnp.float32
        )
        incoming = send_back(dx)
        return (incoming, accum)

    accum0 = jnp.zeros((width, kv_cols), jnp.float32)
    _, accum = lax.fori_loop(0, steps, bstep, (start_buf, accum0))
    grad = lax.psum_scatter(
        accum.astype(jnp.bfloat16), "dp", scatter_dimension=0, tiled=True
    ).astype(jnp.float32)
    total = lax.psum(jnp.sum(grad * grad), ("section", "dp"))
    entries = sections * lax.axis_size("dp") * grad.size
    factor = jnp.minimum(1.0, 0.01 / jnp.sqrt(total / entries))
    scaled = grad * factor
    new_moment = 0.9 * moment[0] + 0.1 * scaled
    new_second = 0.95 * second[0] + 0.05 * scaled * scaled
    new_master = master[0] - 0.002 * new_moment / (jnp.sqrt(new_second) + 1e-08)
    replica = from_behind(new_master.astype(jnp.bfloat16), "section", -1)
    return (new_master[None], new_moment[None], new_second[None], replica[None])


def solution(mesh):
    return jax.shard_map(
        body,
        mesh=mesh,
        in_specs=(
            P(None, "dp", None),
            P(None, "dp", None),
            P(None, "dp"),
            P("section", None),
            P("section", "dp", None),
            P("section", "dp", None),
            P("section", "dp", None),
        ),
        out_specs=(
            P("section", "dp", None),
            P("section", "dp", None),
            P("section", "dp", None),
            P("section", "dp", None),
        ),
        check_vma=False,
    )
```

profile of v0, /device:TPU:1, one launch (start us, length us, event | category | flops | bytes accessed | tf_op | source)
XLA Modules:
  0.0 1035.0 jit_solution(16409207600202464104)
XLA Ops:
  8.9 110.5 %all-gather.2.cloned.1.call-done = bf16[2048,1024]{1,0:T(8,128)(2,1)} async-done(((bf16[64,1024]{1,0:T(8,128)(2,1)}), bf16[2048,1024]{1,0:T(8,128)(2,1)}) %all-gather.2.cloned.1.call-update) | async-done | bytes 4194320 | tf_op jit(solution)/shard_map/all_gather | solution.py:72
  119.5 186.7 %while.34 = (s32[]{:T(128)}, bf16[32,2048]{1,0:T(8,128)(2,1)S(1)}, bf16[4,32,2048]{2,1,0:T(8,128)(2,1)S(1)}, s32[]{:T(128)}, pred[]{:T(512)}, /*index=5*/bf16[4,...) while((s32[]{:T(128)}, bf16[32,2048]{1,0:T(8,128)(2,1)S(1)}, ...), condition=%wide.region_6.7_spmd, body=%wide.region_0.6_spmd.sunk | while | flops 147770976 | bytes 9093281 | solution.py:92
  122.9 7.5 collective-permute-done
  182.9 10.5 %collective-permute-start = (bf16[32,2048]{1,0:T(8,128)(2,1)S(1)}, bf16[32,2048]{1,0:T(8,128)(2,1)S(1)}, u32[]{:S(2)}, u32[]{:S(2)}) collective-permute-start(bf16[32,2048]{1,0:T(8,128)(2,1)S(1)} %get-tuple-element.847), channel_id=1, source_target_pairs={{0,32},{32,64},{64,96},{96,128},{128,160},{160,192},{192,224},{224... | collective-permute-start | bytes 393224 | tf_op jit(solution)/shard_map/while/body/eval_jaxpr/ppermute | solution.py:12
  218.3 11.4 %collective-permute-start = (bf16[32,2048]{1,0:T(8,128)(2,1)S(1)}, bf16[32,2048]{1,0:T(8,128)(2,1)S(1)}, u32[]{:S(2)}, u32[]{:S(2)}) collective-permute-start(bf16[32,2048]{1,0:T(8,128)(2,1)S(1)} %get-tuple-element.847), channel_id=1, source_target_pairs={{0,32},{32,64},{64,96},{96,128},{128,160},{160,192},{192,224},{224... | collective-permute-start | bytes 393224 | tf_op jit(solution)/shard_map/while/body/eval_jaxpr/ppermute | solution.py:12
  306.2 382.2 %while.35 = (s32[]{:T(128)}, bf16[32,2048]{1,0:T(8,128)(2,1)S(1)}, f32[2048,1024]{1,0:T(8,128)}, s32[]{:T(128)}, pred[]{:T(512)}, /*index=5*/bf16[4,32,2048]{2,1...) while((s32[]{:T(128)}, bf16[32,2048]{1,0:T(8,128)(2,1)S(1)}, ...), condition=%wide.region_15.16_spmd.clone, body=%wide.region_7.15_spmd.clone.sunk | while | flops 430495936 | bytes 33964340 | solution.py:125
  317.8 7.9 select_add_fusion.2
  328.4 7.9 select_add_fusion.2
  338.9 7.9 select_add_fusion.2
  349.4 7.9 select_add_fusion.2
  360.0 7.9 select_add_fusion.2
  370.5 7.9 select_add_fusion.2
  381.0 7.9 select_add_fusion.2
  391.6 7.9 select_add_fusion.2
  402.1 7.9 select_add_fusion.2
  412.6 7.9 select_add_fusion.2
  423.2 7.9 select_add_fusion.2
  433.7 7.9 select_add_fusion.2
  444.2 7.9 select_add_fusion.2
  452.2 130.1 %collective-permute-done.1 = bf16[32,2048]{1,0:T(8,128)(2,1)S(1)} collective-permute-done((bf16[32,2048]{1,0:T(8,128)(2,1)S(1)}, bf16[32,2048]{1,0:T(8,128)(2,1)S(1)}, u32[]{:S(2)}, u32[]{:S(2)}) %collective-permute-start.1) | collective-permute-done | bytes 131104 | tf_op jit(solution)/shard_map/while/body/eval_jaxpr/ppermute | solution.py:12
  582.2 12.7 %conditional.6 = (bf16[32,2048]{1,0:T(8,128)(2,1)S(1)}, bf16[32,2048]{1,0:T(8,128)(2,1)S(1)}, bf16[32,1024]{1,0:T(8,128)(2,1)}) conditional(s32[]{:T(128)} %convert_element_type.270, () %tuple.118, (pred[]{:T(512)}, s32[]{:T(128)}, bf16[4,32,2048]{2,1,0:T(8,128)(2,1)}, bf16[32,2048]{1,0:T(8,128)(2,1)S(1)}, s32[4,32]{1,0:T(4,128)}, ...), branch_computations={%region_8.8_spmd, %region_9.14_spmd} | conditional | flops 292083904 | bytes 16465953 | solution.py:104
  596.9 7.9 select_add_fusion.2
  604.8 12.7 %conditional.6 = (bf16[32,2048]{1,0:T(8,128)(2,1)S(1)}, bf16[32,2048]{1,0:T(8,128)(2,1)S(1)}, bf16[32,1024]{1,0:T(8,128)(2,1)}) conditional(s32[]{:T(128)} %convert_element_type.270, () %tuple.118, (pred[]{:T(512)}, s32[]{:T(128)}, bf16[4,32,2048]{2,1,0:T(8,128)(2,1)}, bf16[32,2048]{1,0:T(8,128)(2,1)S(1)}, s32[4,32]{1,0:T(4,128)}, ...), branch_computations={%region_8.8_spmd, %region_9.14_spmd} | conditional | flops 292083904 | bytes 16465953 | solution.py:104
  619.4 7.9 select_add_fusion.2
  627.3 12.7 %conditional.6 = (bf16[32,2048]{1,0:T(8,128)(2,1)S(1)}, bf16[32,2048]{1,0:T(8,128)(2,1)S(1)}, bf16[32,1024]{1,0:T(8,128)(2,1)}) conditional(s32[]{:T(128)} %convert_element_type.270, () %tuple.118, (pred[]{:T(512)}, s32[]{:T(128)}, bf16[4,32,2048]{2,1,0:T(8,128)(2,1)}, bf16[32,2048]{1,0:T(8,128)(2,1)S(1)}, s32[4,32]{1,0:T(4,128)}, ...), branch_computations={%region_8.8_spmd, %region_9.14_spmd} | conditional | flops 292083904 | bytes 16465953 | solution.py:104
  642.0 7.9 select_add_fusion.2
  649.9 12.7 %conditional.6 = (bf16[32,2048]{1,0:T(8,128)(2,1)S(1)}, bf16[32,2048]{1,0:T(8,128)(2,1)S(1)}, bf16[32,1024]{1,0:T(8,128)(2,1)}) conditional(s32[]{:T(128)} %convert_element_type.270, () %tuple.118, (pred[]{:T(512)}, s32[]{:T(128)}, bf16[4,32,2048]{2,1,0:T(8,128)(2,1)}, bf16[32,2048]{1,0:T(8,128)(2,1)S(1)}, s32[4,32]{1,0:T(4,128)}, ...), branch_computations={%region_8.8_spmd, %region_9.14_spmd} | conditional | flops 292083904 | bytes 16465953 | solution.py:104
  664.5 7.9 select_add_fusion.2
  673.1 7.3 collective-permute-start.1
  680.4 7.9 select_add_fusion.2
  694.4 222.8 %reduce-scatter.2.cloned.1.call-done = bf16[64,1024]{1,0:T(8,128)(2,1)} async-done(((bf16[2048,1024]{1,0:T(8,128)(2,1)}), bf16[64,1024]{1,0:T(8,128)(2,1)}) %reduce-scatter.2.cloned.1.call-update) | async-done | bytes 131088 | tf_op jit(solution)/shard_map/reduce_scatter | solution.py:126
  918.8 99.8 %psum.7 = f32[]{:T(128)} all-reduce(f32[]{:T(128)} %fusion.63), channel_id=1, replica_groups=mesh['section'=16,'dp'=32] {'section','dp'}, use_global_device_ids=true, to_apply=%region_18.19 | all-reduce | flops 1 | bytes 8 | tf_op jit(solution)/shard_map/psum | solution.py:129
  (429 shorter events, 310.8 us)
Async XLA Ops:
  7.2 112.2 %all-gather.2.cloned.1.call-start = ((), (), s32[]{:S(2)}) async-start(), calls=%async_computation.1 | async-start | bytes 4325376 | tf_op jit(solution)/shard_map/all_gather | solution.py:72
  8.9 908.4 %reduce-scatter.2.cloned.1.call-start = ((), (), s32[]{:S(2)}) async-start(), calls=%async_computation.2 | async-start | bytes 4325376 | tf_op jit(solution)/shard_map/reduce_scatter | solution.py:126
  120.5 9.9 collective-permute-start
  182.9 12.4 %collective-permute-start = (bf16[32,2048]{1,0:T(8,128)(2,1)S(1)}, bf16[32,2048]{1,0:T(8,128)(2,1)S(1)}, u32[]{:S(2)}, u32[]{:S(2)}) collective-permute-start(bf16[32,2048]{1,0:T(8,128)(2,1)S(1)} %get-tuple-element.847), channel_id=1, source_target_pairs={{0,32},{32,64},{64,96},{96,128},{128,160},{160,192},{192,224},{224... | collective-permute-start | bytes 393224 | tf_op jit(solution)/shard_map/while/body/eval_jaxpr/ppermute | solution.py:12
  218.3 13.3 %collective-permute-start = (bf16[32,2048]{1,0:T(8,128)(2,1)S(1)}, bf16[32,2048]{1,0:T(8,128)(2,1)S(1)}, u32[]{:S(2)}, u32[]{:S(2)}) collective-permute-start(bf16[32,2048]{1,0:T(8,128)(2,1)S(1)} %get-tuple-element.847), channel_id=1, source_target_pairs={{0,32},{32,64},{64,96},{96,128},{128,160},{160,192},{192,224},{224... | collective-permute-start | bytes 393224 | tf_op jit(solution)/shard_map/while/body/eval_jaxpr/ppermute | solution.py:12
  232.7 7.2 collective-permute-start
  240.9 7.2 collective-permute-start
  249.1 7.2 collective-permute-start
  257.3 7.2 collective-permute-start
  265.5 7.2 collective-permute-start
  273.7 7.2 collective-permute-start
  281.9 7.2 collective-permute-start
  290.2 7.8 collective-permute-start
  306.9 8.3 collective-permute-start.1
  315.9 9.9 collective-permute-start.1
  326.4 9.9 collective-permute-start.1
  337.0 9.9 collective-permute-start.1
  347.5 9.9 collective-permute-start.1
  358.0 9.9 collective-permute-start.1
  368.6 9.9 collective-permute-start.1
  379.1 9.9 collective-permute-start.1
  389.6 9.9 collective-permute-start.1
  400.2 9.9 collective-permute-start.1
  410.7 9.9 collective-permute-start.1
  421.2 9.9 collective-permute-start.1
  431.8 9.9 collective-permute-start.1
  442.3 139.9 %collective-permute-start.1 = (bf16[32,2048]{1,0:T(8,128)(2,1)S(1)}, bf16[32,2048]{1,0:T(8,128)(2,1)S(1)}, u32[]{:S(2)}, u32[]{:S(2)}) collective-permute-start(bf16[32,2048]{1,0:T(8,128)(2,1)S(1)} %get-tuple-element.752), channel_id=1, source_target_pairs={{32,0},{64,32},{96,64},{128,96},{160,128},{192,160},{224,192},{256... | collective-permute-start | bytes 393224 | tf_op jit(solution)/shard_map/while/body/eval_jaxpr/ppermute | solution.py:12
  594.9 9.9 collective-permute-start.1
  617.5 9.9 collective-permute-start.1
  640.0 9.9 collective-permute-start.1
  662.6 9.9 collective-permute-start.1
  673.1 15.3 %collective-permute-start.1 = (bf16[32,2048]{1,0:T(8,128)(2,1)S(1)}, bf16[32,2048]{1,0:T(8,128)(2,1)S(1)}, u32[]{:S(2)}, u32[]{:S(2)}) collective-permute-start(bf16[32,2048]{1,0:T(8,128)(2,1)S(1)} %get-tuple-element.752), channel_id=1, source_target_pairs={{32,0},{64,32},{96,64},{128,96},{160,128},{192,160},{224,192},{256... | collective-permute-start | bytes 393224 | tf_op jit(solution)/shard_map/while/body/eval_jaxpr/ppermute | solution.py:12
  (24 other events, 1092.7 us)
Sparse Core Ops, SparseCore 0:
  11.7 107.6 all-gather.1
  694.5 222.6 reduce-scatter.1
where the time goes:
time: 1040 us
  waiting for transfers between devices  510 us (49%)
  matrix products  197 us (19%)
  starting transfers between devices  145 us (14%)
  blocking collectives  99.8 us (10%)
  other arithmetic  45.2 us (4%)
  local copies, waits for them, and re-layouts  20.9 us (2%)
  between operations  14.8 us (1%)
    reduce_scatter x1, waiting for transfers between devices, body(): lax.psum_scatter(accum.astype(jnp.bfloat16), 'dp', scatter_dimension=0, t...  223 us
    ppermute x38, waiting for transfers between devices, shifted(): return lax.ppermute(block, axis, route)  173 us
    dot_general x19, matrix products, bstep(): lax.dot_general(hb, dkv, (((0,), (0,)), ((), ())), preferred_element_type...  148 us
    ppermute x38, starting transfers between devices, shifted(): return lax.ppermute(block, axis, route)  142 us
    all_gather x1, waiting for transfers between devices, body(): lax.all_gather(master[0].astype(jnp.bfloat16), 'dp', axis=0, tiled=True)  110 us
    psum x1, blocking collectives, body(): total = lax.psum(jnp.sum(grad * grad), ('section', 'dp'))  99.8 us
  transfers between devices with their start and end apart: 41, of which 24 were waited for; matrix products, arithmetic and copies ran while one was open for 14% of the time, Pallas kernels for 0%

commit v1 on v0

v1 whole, which is shorter than its diff:
```python
import functools

import jax
import jax.numpy as jnp
from jax import lax
from jax.experimental import pallas as pl
from jax.experimental.pallas import tpu as pltpu
from jax.sharding import Mesh
from jax.sharding import PartitionSpec as P

HEAD = 128
X, ZL, C, Y, ZH = 4, 2, 2, 8, 4
AXES = ("x", "zl", "c", "y", "zh")
SECTION = ("x", "zl", "c")
DP = ("y", "zh")
LAYERS = ZL * C
RING = 8
OFFSETS = (0, 1, -1, 2, -2, 3, -3, 4)
KV_HEADS = 4
GROUPS = 4
F32 = jnp.float32
BF16 = jnp.bfloat16


def flat(x, zl, c, y, zh):
    return (((x * ZL + zl) * C + c) * Y + y) * ZH + zh


def everywhere(target):
    pairs = []
    for x in range(X):
        for zl in range(ZL):
            for c in range(C):
                for y in range(Y):
                    for zh in range(ZH):
                        pairs.append((flat(x, zl, c, y, zh), flat(*target(x, zl, c, y, zh))))
    return pairs


def swap_route(bit):
    def target(x, zl, c, y, zh):
        if c == 1:
            return (x, zl, c, y ^ (1 << bit), zh)
        if bit == 0:
            return (x, zl ^ 1, c, y, zh)
        return (x, zl, c, y, zh ^ (1 << (bit - 1)))

    return everywhere(target)


def ring_route(step):
    def target(x, zl, c, y, zh):
        if c == 0:
            return (x, zl, c, (y + step) % Y, zh)
        z = (2 * zh + zl + step) % (ZL * ZH)
        return (x, z % 2, c, y, z // 2)

    return everywhere(target)


def gathered_weights(own):
    c, y = lax.axis_index("c"), lax.axis_index("y")
    zl, zh = lax.axis_index("zl"), lax.axis_index("zh")
    rows, cols = own.shape
    bits = (
        jnp.where(c == 1, y // 4, zh // 2),
        jnp.where(c == 1, (y // 2) % 2, zh % 2),
        jnp.where(c == 1, y % 2, zl),
    )
    piece = own[None]
    for bit, mine, axis in ((2, bits[0], 0), (1, bits[1], 1), (0, bits[2], 0)):
        other = lax.ppermute(piece, AXES, swap_route(bit))
        low, high = jnp.where(mine == 0, piece, other), jnp.where(mine == 0, other, piece)
        if axis == 0:
            piece = jnp.concatenate([low, high], axis=0)
        else:
            piece = jnp.stack([low, high], axis=1).reshape(-1, rows, cols)
    pieces = [piece]
    up = down = piece
    for step in range(1, 5):
        up = lax.ppermute(up, AXES, ring_route(1))
        pieces.append(up)
        if step < 4:
            down = lax.ppermute(down, AXES, ring_route(-1))
            pieces.append(down)
    others = [lax.ppermute(p, "c", [(0, 1), (1, 0)]) for p in pieces]
    return pieces + others


def fetch_weights(pieces, w, sems):
    c, y = lax.axis_index("c"), lax.axis_index("y")
    z = 2 * lax.axis_index("zh") + lax.axis_index("zl")

    def start(first, second):
        for i, offset in enumerate(OFFSETS):
            there = lax.rem(y - offset + 2 * RING, RING)
            for low in range(2):
                pltpu.make_async_copy(
                    first[i].at[pl.ds(4 * low, 4)],
                    w.at[2 * low, there // 2, lax.rem(there, 2)],
                    sems.at[2 * low],
                ).start()
        for i, offset in enumerate(OFFSETS):
            there = lax.rem(z - offset + 2 * RING, RING)
            layer = 2 * lax.rem(there, 2) + 1
            for low in range(2):
                pltpu.make_async_copy(
                    second[i].at[pl.ds(4 * low, 4)],
                    w.at[layer, :, low, there // 2],
                    sems.at[layer],
                ).start()

    @pl.when(c == 0)
    def _():
        start(pieces[:RING], pieces[RING:])

    @pl.when(c == 1)
    def _():
        start(pieces[RING:], pieces[:RING])


def wait_weights(w, sems, layer):
    pltpu.make_async_copy(w.at[layer], w.at[layer], sems.at[layer]).wait()


def cols(index):
    return pl.ds(index * HEAD, HEAD)


def stacked(ref, layer, group):
    parts = [ref[layer, :, cols(group * GROUPS + a)] for a in range(GROUPS)]
    return jnp.concatenate(parts, axis=0)


def forward_kernel(x_ref, gain_ref, mask_ref, *rest):
    pieces = rest[: 2 * RING]
    y_ref, xs_ref, h_ref, kv_ref, p_ref, w, sems = rest[2 * RING :]
    fetch_weights(pieces, w, sems)
    length, width = x_ref.shape
    y_ref[...] = x_ref[...]

    @pl.loop(0, LAYERS)
    def _(layer):
        xs_ref[layer] = y_ref[...]
        xf = y_ref[...].astype(F32)
        scale = lax.rsqrt(jnp.mean(xf * xf, axis=-1, keepdims=True) + 1e-05)
        h_ref[layer] = (xf * scale * gain_ref[layer]).astype(BF16)
        wait_weights(w, sems, layer)
        whole = w[layer].reshape(width, -1)
        kv_ref[layer] = jnp.dot(h_ref[layer], whole, preferred_element_type=F32).astype(BF16)
        for g in range(KV_HEADS):
            query = stacked(h_ref, layer, g)
            key = kv_ref[layer, :, cols(g)]
            value = kv_ref[layer, :, cols(KV_HEADS + g)]
            s = lax.dot_general(key, query, (((1,), (1,)), ((), ())), preferred_element_type=F32)
            s = jnp.where(mask_ref[...] > 0, s * HEAD ** (-0.5), -1e30)
            e = jnp.exp(s - jnp.max(s, axis=0, keepdims=True))
            p = e / jnp.sum(e, axis=0, keepdims=True)
            p_ref[layer, :, cols(g)] = p
            o = lax.dot_general(
                p.astype(BF16), value, (((0,), (0,)), ((), ())), preferred_element_type=F32
            )
            for a in range(GROUPS):
                at = cols(g * GROUPS + a)
                y_ref[:, at] = (
                    xs_ref[layer, :, at].astype(F32) + o[a * length : (a + 1) * length]
                ).astype(BF16)


def backward_kernel(dy_ref, gain_ref, xs_ref, h_ref, kv_ref, p_ref, *rest):
    pieces = rest[: 2 * RING]
    dx_ref, dkv_ref, w, sems, dh_ref = rest[2 * RING :]
    fetch_weights(pieces, w, sems)
    length, width = dy_ref.shape
    dx_ref[...] = dy_ref[...]

    @pl.loop(0, LAYERS)
    def _(turn):
        layer = LAYERS - 1 - turn
        for g in range(KV_HEADS):
            query = stacked(h_ref, layer, g)
            key = kv_ref[layer, :, cols(g)]
            value = kv_ref[layer, :, cols(KV_HEADS + g)]
            p = p_ref[layer, :, cols(g)]
            do = jnp.concatenate(
                [dx_ref[:, cols(g * GROUPS + a)] for a in range(GROUPS)], axis=0
            )
            dv = jnp.dot(p.astype(BF16), do, preferred_element_type=F32)
            dp = lax.dot_general(value, do, (((1,), (1,)), ((), ())), preferred_element_type=F32)
            ds = p * (dp - jnp.sum(p * dp, axis=0, keepdims=True)) * HEAD ** (-0.5)
            ds = ds.astype(BF16)
            dk = jnp.dot(ds, query, preferred_element_type=F32)
            dq = lax.dot_general(ds, key, (((0,), (0,)), ((), ())), preferred_element_type=F32)
            dkv_ref[layer, :, cols(g)] = dk.astype(BF16)
            dkv_ref[layer, :, cols(KV_HEADS + g)] = dv.astype(BF16)
            for a in range(GROUPS):
                dh_ref[:, cols(g * GROUPS + a)] = dq[a * length : (a + 1) * length]
        wait_weights(w, sems, layer)
        whole = w[layer].reshape(width, -1)
        dh = dh_ref[...] + lax.dot_general(
            dkv_ref[layer], whole, (((1,), (1,)), ((), ())), preferred_element_type=F32
        )
        xf = xs_ref[layer].astype(F32)
        scale = lax.rsqrt(jnp.mean(xf * xf, axis=-1, keepdims=True) + 1e-05)
        gd = dh * gain_ref[layer]
        along = jnp.mean(xf * gd, axis=-1, keepdims=True) * (scale * scale * scale)
        dx_ref[...] = (dx_ref[...].astype(F32) + (gd * scale - xf * along)).astype(BF16)


def weights_scratch(pieces):
    rows, columns = pieces[0].shape[1:]
    return [
        pltpu.VMEM((LAYERS, Y // 2, 2, ZH, rows, columns), BF16),
        pltpu.SemaphoreType.DMA((LAYERS,)),
    ]


VMEM = pl.BlockSpec(memory_space=pltpu.VMEM)
ANY = pl.BlockSpec(memory_space=pl.ANY)
PARAMS = dict(vmem_limit_bytes=48 * 1024 * 1024)


def run_forward(x, gains, mask, pieces):
    length, width = x.shape
    columns = pieces[0].shape[2]
    return pl.pallas_call(
        forward_kernel,
        out_shape=(
            jax.ShapeDtypeStruct((length, width), BF16),
            jax.ShapeDtypeStruct((LAYERS, length, width), BF16),
            jax.ShapeDtypeStruct((LAYERS, length, width), BF16),
            jax.ShapeDtypeStruct((LAYERS, length, columns), BF16),
            jax.ShapeDtypeStruct((LAYERS, length, KV_HEADS * HEAD), F32),
        ),
        in_specs=[VMEM] * 3 + [ANY] * (2 * RING),
        out_specs=(VMEM,) * 5,
        scratch_shapes=weights_scratch(pieces),
        compiler_params=pltpu.CompilerParams(**PARAMS),
        name="stage_forward",
    )(x, gains, mask, *pieces)


def run_backward(dy, gains, saved, pieces):
    length, width = dy.shape
    columns = pieces[0].shape[2]
    return pl.pallas_call(
        backward_kernel,
        out_shape=(
            jax.ShapeDtypeStruct((length, width), BF16),
            jax.ShapeDtypeStruct((LAYERS, length, columns), BF16),
        ),
        in_specs=[VMEM] * 6 + [ANY] * (2 * RING),
        out_specs=(VMEM,) * 2,
        scratch_shapes=weights_scratch(pieces) + [pltpu.VMEM((length, width), F32)],
        compiler_params=pltpu.CompilerParams(**PARAMS),
        name="stage_backward",
    )(dy, gains, *saved, *pieces)


def exchange(block, axes):
    return lax.all_to_all(block, axes, split_axis=0, concat_axis=0, tiled=True)


def total_of(value):
    for axes, count in ((DP, Y * ZH), (SECTION, X * ZL * C)):
        sent = jnp.broadcast_to(value.reshape(1, 1), (count, 128))
        value = jnp.sum(exchange(sent, axes)[:, 0])
    return value


def body(inputs, upstream, segments, gains, master, moment, second):
    stage = lax.axis_index("x")
    which = lax.axis_index("zl") * C + lax.axis_index("c")
    length, width = inputs.shape[1:]
    rows, columns = master.shape[1:]

    pieces = gathered_weights(master[0].astype(BF16))
    plane_gains = lax.all_gather(gains, ("zl", "c"), axis=0)
    seg = lax.dynamic_index_in_dim(segments, which, 0, keepdims=False)
    place = jnp.arange(length)
    allowed = (place[None, :] >= place[:, None]) & (seg[None, :] == seg[:, None])
    mask = jnp.tile(allowed.astype(F32), (1, GROUPS))
    first = lax.dynamic_index_in_dim(inputs, which, 0, keepdims=False)
    last = lax.dynamic_index_in_dim(upstream, which, 0, keepdims=False)

    held = first
    for turn in range(X):
        y, *saved = run_forward(held, plane_gains, mask, pieces)
        if turn < X - 1:
            arrived = lax.ppermute(y, "x", [(turn, turn + 1)])
            held = jnp.where(stage == turn + 1, arrived, held)
    h = saved[1]
    layer_h = exchange(h, ("zl", "c")).reshape(LAYERS * length, width)
    all_h = lax.all_gather(layer_h, "y", axis=0, tiled=True)

    held = last
    for turn in range(X):
        dx, dkv = run_backward(held, plane_gains, saved, pieces)
        if turn < X - 1:
            here = X - 1 - turn
            arrived = lax.ppermute(dx, "x", [(here, here - 1)])
            held = jnp.where(stage == here - 1, arrived, held)

    sent = dkv.reshape(LAYERS, length, Y, columns // Y).transpose(0, 2, 1, 3)
    sent = sent.reshape(LAYERS * Y, length, columns // Y)
    got = exchange(sent, ("zl", "c", "y")).reshape(LAYERS, Y, length, columns // Y)
    tokens = got.transpose(1, 0, 2, 3).reshape(Y * LAYERS * length, columns // Y)
    partial = lax.dot_general(
        all_h, tokens, (((0,), (0,)), ((), ())), preferred_element_type=F32
    ).astype(BF16)
    got = exchange(partial.reshape(Y * ZH, rows, columns // Y), DP)
    grad = jnp.sum(got.reshape(Y, ZH, rows, columns // Y).astype(F32), axis=1)
    grad = grad.transpose(1, 0, 2).reshape(rows, columns)

    total = total_of(jnp.sum(grad * grad))
    entries = X * ZL * C * Y * ZH * grad.size
    factor = jnp.minimum(1.0, 0.01 / jnp.sqrt(total / entries))
    scaled = grad * factor
    new_moment = 0.9 * moment[0] + 0.1 * scaled
    new_second = 0.95 * second[0] + 0.05 * scaled * scaled
    new_master = master[0] - 0.002 * new_moment / (jnp.sqrt(new_second) + 1e-08)
    sections = X * ZL * C
    route = [((i + 1) % sections, i) for i in range(sections)]
    replica = lax.ppermute(new_master.astype(BF16), SECTION, route)
    return (new_master[None], new_moment[None], new_second[None], replica[None])


def solution(mesh):
    fine = Mesh(mesh.devices.reshape(X, ZL, C, Y, ZH), AXES)
    state = P(SECTION, DP, None)
    return jax.shard_map(
        body,
        mesh=fine,
        in_specs=(
            P(None, DP, None),
            P(None, DP, None),
            P(None, DP),
            P(SECTION, None),
            state,
            state,
            state,
        ),
        out_specs=(state,) * 4,
        check_vma=False,
    )
```

time: 1040 us -> 389 us (0.37)
  waiting for transfers between devices: 510 us -> 71.6 us
  matrix products: 197 us -> 3.57 us
  Pallas kernels: 0 us -> 103 us
  starting transfers between devices: 145 us -> 82.7 us
  other arithmetic: 45.2 us -> 6.54 us
    reduce_scatter x1 -> x0, waiting for transfers between devices: 223 us -> none  [body(): lax.psum_scatter(accum.astype(jnp.bfloat16), 'dp', scatter_dimension=0, t...]
    dot_general x59 -> x1, matrix products: 195 us -> 3.57 us  [body(): lax.dot_general(all_h, tokens, (((0,), (0,)), ((), ())), preferred_elemen...]
    all_gather x1, waiting for transfers between devices: 110 us -> 0.02 us  [body(): all_h = lax.all_gather(layer_h, 'y', axis=0, tiled=True)]
    ppermute x39 -> x25, waiting for transfers between devices: 177 us -> 71.5 us  [the longest x4 25.4 us: gathered_weights(): up = lax.ppermute(up, AXES, ring_route(1))]
    pallas_call x0 -> x8, Pallas kernels: none -> 103 us  [the longest x4 56.2 us: run_backward(): pl.pallas_call(backward_kernel, out_shape=(jax.ShapeDtypeStruct((length,...]
    psum x1 -> x0, blocking collectives: 99.8 us -> none  [body(): total = lax.psum(jnp.sum(grad * grad), ('section', 'dp'))]
    all_to_all x0 -> x5, blocking collectives: none -> 88.7 us  [exchange(): return lax.all_to_all(block, axes, split_axis=0, concat_axis=0, tiled=True)]
    ppermute x39 -> x25, starting transfers between devices: 145 us -> 82.7 us  [the longest x8 25.1 us: gathered_weights(): others = [lax.ppermute(p, 'c', [(0, 1), (1, 0)]) for p in pieces]]
  transfers between devices with their start and end apart: 41 -> 26, of which waited for: 24 -> 11; matrix products, arithmetic and copies ran while one was open for 14% -> 1% of each run, Pallas kernels for 0% -> 14%
where the time goes in v1:
time: 389 us; the launch traced here: 388 us
  Pallas kernels  103 us (26%)
  blocking collectives  93.8 us (24%)
  starting transfers between devices  82.7 us (21%)
  waiting for transfers between devices  71.6 us (18%)
  between operations  15.5 us (4%)
  local copies, waits for them, and re-layouts  11.8 us (3%)
  other arithmetic  6.54 us (2%)
    all_to_all x5, blocking collectives, exchange(): return lax.all_to_all(block, axes, split_axis=0, concat_axis=0, tiled=True)  88.7 us
    pallas_call x4, Pallas kernels, run_backward(): pl.pallas_call(backward_kernel, out_shape=(jax.ShapeDtypeStruct((length,...  56.2 us
    pallas_call x4, Pallas kernels, run_forward(): pl.pallas_call(forward_kernel, out_shape=(jax.ShapeDtypeStruct((length, w...  46.4 us
    ppermute x4, waiting for transfers between devices, gathered_weights(): up = lax.ppermute(up, AXES, ring_route(1))  25.4 us
    ppermute x8, starting transfers between devices, gathered_weights(): others = [lax.ppermute(p, 'c', [(0, 1), (1, 0)]) for p in pieces]  25.1 us
    ppermute x3, waiting for transfers between devices, body(): arrived = lax.ppermute(dx, 'x', [(here, here - 1)])  24.3 us
    ppermute x3, starting transfers between devices, gathered_weights(): down = lax.ppermute(down, AXES, ring_route(-1))  20 us
    ppermute x3, waiting for transfers between devices, gathered_weights(): other = lax.ppermute(piece, AXES, swap_route(bit))  16.6 us
  transfers between devices with their start and end apart: 26, of which 11 were waited for; matrix products, arithmetic and copies ran while one was open for 1% of the time, Pallas kernels for 14%

profile of v1, /device:TPU:1, one launch (start us, length us, event | category | flops | bytes accessed | tf_op | source)
XLA Modules:
  0.0 388.0 jit_solution(7623827823170351968)
XLA Ops:
  8.2 8.3 %collective-permute-start = (bf16[1,64,1024]{2,1,0:T(8,128)(2,1)S(1)}, bf16[1,64,1024]{2,1,0:T(8,128)(2,1)S(1)}, u32[]{:S(2)}, u32[]{:S(2)}) collective-permute-start(bf16[1,64,1024]{2,1,0:T(8,128)(2,1)S(1)} %convert_element_type.24), channel_id=1, source_target_pairs={{0,2},{1,3},{2,0},{3,1},{4,6},{5,7},{6,4},{7,5},{8,10},{9,11},{10,... | collective-permute-start | bytes 393224 | tf_op jit(solution)/shard_map/ppermute | solution.py:72
  20.0 5.4 %collective-permute-start.1 = (bf16[2,64,1024]{2,1,0:T(8,128)(2,1)S(1)}, bf16[2,64,1024]{2,1,0:T(8,128)(2,1)S(1)}, u32[]{:S(2)}, u32[]{:S(2)}) collective-permute-start(bf16[2,64,1024]{2,1,0:T(8,128)(2,1)S(1)} %pad_maximum_fusion.2), channel_id=1, source_target_pairs={{0,1},{1,0},{2,3},{3,2},{4,5},{5,4},{6,7},{7,6},{8,9},{9,8},{10,11... | collective-permute-start | bytes 786440 | tf_op jit(solution)/shard_map/ppermute | solution.py:72
  25.4 6.2 %collective-permute-done.1 = bf16[2,64,1024]{2,1,0:T(8,128)(2,1)S(1)} collective-permute-done((bf16[2,64,1024]{2,1,0:T(8,128)(2,1)S(1)}, bf16[2,64,1024]{2,1,0:T(8,128)(2,1)S(1)}, u32[]{:S(2)}, u32[]{:S(2)}) %collective-permute-start.1) | collective-permute-done | bytes 262176 | tf_op jit(solution)/shard_map/ppermute | solution.py:72
  33.7 8.0 %collective-permute-done.2 = bf16[4,64,1024]{2,1,0:T(8,128)(2,1)S(1)} collective-permute-done((bf16[4,64,1024]{2,1,0:T(8,128)(2,1)S(1)}, bf16[4,64,1024]{2,1,0:T(8,128)(2,1)S(1)}, u32[]{:S(2)}, u32[]{:S(2)}) %collective-permute-start.2) | collective-permute-done | bytes 524320 | tf_op jit(solution)/shard_map/ppermute | solution.py:72
  42.0 4.6 %collective-permute-start.3 = (bf16[8,64,1024]{2,1,0:T(8,128)(2,1)S(1)}, bf16[8,64,1024]{2,1,0:T(8,128)(2,1)S(1)}, u32[]{:S(2)}, u32[]{:S(2)}) collective-permute-start(bf16[8,64,1024]{2,1,0:T(8,128)(2,1)S(1)} %pad_maximum_fusion.rest_0_), channel_id=1, source_target_pairs={{0,4},{1,5},{2,6},{3,7},{4,8},{5,9},{6,10},{7,11},{8,12},{9,13},{1... | collective-permute-start | bytes 3145736 | tf_op jit(solution)/shard_map/ppermute | solution.py:81
  46.5 8.8 %collective-permute-start.4 = (bf16[8,64,1024]{2,1,0:T(8,128)(2,1)S(1)}, bf16[8,64,1024]{2,1,0:T(8,128)(2,1)S(1)}, u32[]{:S(2)}, u32[]{:S(2)}) collective-permute-start(bf16[8,64,1024]{2,1,0:T(8,128)(2,1)S(1)} %pad_maximum_fusion.rest_0_), channel_id=1, source_target_pairs={{0,28},{1,29},{2,30},{3,31},{4,0},{5,1},{6,2},{7,3},{8,4},{9,5},{1... | collective-permute-start | bytes 3145736 | tf_op jit(solution)/shard_map/ppermute | solution.py:84
  55.3 10.5 %collective-permute-done.3.rest_1_ = bf16[8,64,1024]{2,1,0:T(8,128)(2,1)S(1)} collective-permute-done((bf16[8,64,1024]{2,1,0:T(8,128)(2,1)S(1)}, bf16[8,64,1024]{2,1,0:T(8,128)(2,1)S(1)}, u32[]{:S(2)}, u32[]{:S(2)}) %collective-permute-start.3) | collective-permute-done | bytes 1048608 | tf_op jit(solution)/shard_map/ppermute | solution.py:81
  67.8 4.6 %collective-permute-start.6 = (bf16[8,64,1024]{2,1,0:T(8,128)(2,1)S(1)}, bf16[8,64,1024]{2,1,0:T(8,128)(2,1)}, u32[]{:S(2)}, u32[]{:S(2)}) collective-permute-start(bf16[8,64,1024]{2,1,0:T(8,128)(2,1)S(1)} %collective-permute-done.4.rest_2_), channel_id=1, source_target_pairs={{0,28},{1,29},{2,30},{3,31},{4,0},{5,1},{6,2},{7,3},{8,4},{9,5},{1... | collective-permute-start | bytes 3145736 | tf_op jit(solution)/shard_map/ppermute | solution.py:84
  72.4 10.6 %collective-permute-done.5.rest_3_ = bf16[8,64,1024]{2,1,0:T(8,128)(2,1)} collective-permute-done((bf16[8,64,1024]{2,1,0:T(8,128)(2,1)S(1)}, bf16[8,64,1024]{2,1,0:T(8,128)(2,1)}, u32[]{:S(2)}, u32[]{:S(2)}) %collective-permute-start.5) | collective-permute-done | bytes 1048608 | tf_op jit(solution)/shard_map/ppermute | solution.py:81
  84.9 4.0 %collective-permute-start.10 = (bf16[8,64,1024]{2,1,0:T(8,128)(2,1)S(1)}, bf16[8,64,1024]{2,1,0:T(8,128)(2,1)S(1)}, u32[]{:S(2)}, u32[]{:S(2)}) collective-permute-start(bf16[8,64,1024]{2,1,0:T(8,128)(2,1)S(1)} %pad_maximum_fusion.rest_0_), channel_id=1, source_target_pairs={{0,32},{32,0},{1,33},{33,1},{2,34},{34,2},{3,35},{35,3},{4,36},{36... | collective-permute-start | bytes 3145736 | tf_op jit(solution)/shard_map/ppermute | solution.py:86
  93.3 6.7 %collective-permute-start.8 = (bf16[8,64,1024]{2,1,0:T(8,128)(2,1)}, bf16[8,64,1024]{2,1,0:T(8,128)(2,1)}, u32[]{:S(2)}, u32[]{:S(2)}) collective-permute-start(bf16[8,64,1024]{2,1,0:T(8,128)(2,1)} %collective-permute-done.6.rest_4_), channel_id=1, source_target_pairs={{0,28},{1,29},{2,30},{3,31},{4,0},{5,1},{6,2},{7,3},{8,4},{9,5},{1... | collective-permute-start | bytes 3145736 | tf_op jit(solution)/shard_map/ppermute | solution.py:84
  102.3 4.8 %collective-permute-start.13 = (bf16[8,64,1024]{2,1,0:T(8,128)(2,1)}, bf16[8,64,1024]{2,1,0:T(8,128)(2,1)}, u32[]{:S(2)}, u32[]{:S(2)}) collective-permute-start(bf16[8,64,1024]{2,1,0:T(8,128)(2,1)} %collective-permute-done.5.rest_3_), channel_id=1, source_target_pairs={{0,32},{32,0},{1,33},{33,1},{2,34},{34,2},{3,35},{35,3},{4,36},{36... | collective-permute-start | bytes 3145736 | tf_op jit(solution)/shard_map/ppermute | solution.py:86
  113.9 3.8 collective-permute-done.9.rest_7_
  117.7 5.7 %collective-permute-start.17 = (bf16[8,64,1024]{2,1,0:T(8,128)(2,1)}, bf16[8,64,1024]{2,1,0:T(8,128)(2,1)}, u32[]{:S(2)}, u32[]{:S(2)}) collective-permute-start(bf16[8,64,1024]{2,1,0:T(8,128)(2,1)} %collective-permute-done.9.rest_7_), channel_id=1, source_target_pairs={{0,32},{32,0},{1,33},{33,1},{2,34},{34,2},{3,35},{35,3},{4,36},{36... | collective-permute-start | bytes 3145736 | tf_op jit(solution)/shard_map/ppermute | solution.py:86
  123.7 5.0 %all-gather.1.gain_ref = f32[4,1,2048]{2,1,0:T(1,128)S(1)} all-gather(f32[1,1,2048]{2,1,0:T(1,128)S(1)} %bitcast.72), channel_id=2, replica_groups=mesh['x'=4,'zl'=2,'c'=2,'y'=8,'zh'=4] {'zl','c'}, dimensions={0}, use_global_device_ids=true | all-gather | bytes 40960 | tf_op jit(solution)/shard_map/all_gather | solution.py:278
  130.3 11.6 %stage_forward.4 = (bf16[32,2048]{1,0:T(8,128)(2,1)S(1)}, bf16[4,32,2048]{2,1,0:T(8,128)(2,1)}, bf16[4,32,2048]{2,1,0:T(8,128)(2,1)}, bf16[4,32,1024]{2,1,0:T(8,128)(2,1)}, f32[4,32,512]{2,1,0:T(8,128)}) custom-call(bf16[32,2048]{1,0:T(8,128)(2,1)S(1)} %get-tuple-element.38.x_ref, f32[4,1,2048]{2,1,0:T(1,128)S(1)} %all-gather.1.gain_ref, ...), custom_call_target="tpu_custom_call" | custom-call | tf_op jit(solution)/shard_map/stage_forward/pallas_call | solution.py:226
  141.9 3.8 collective-permute-start.18
  147.8 11.6 %stage_forward.5 = (bf16[32,2048]{1,0:T(8,128)(2,1)S(1)}, bf16[4,32,2048]{2,1,0:T(8,128)(2,1)}, bf16[4,32,2048]{2,1,0:T(8,128)(2,1)}, bf16[4,32,1024]{2,1,0:T(8,128)(2,1)}, f32[4,32,512]{2,1,0:T(8,128)}) custom-call(bf16[32,2048]{1,0:T(8,128)(2,1)S(1)} %broadcast_select_fusion.6.x_ref, f32[4,1,2048]{2,1,0:T(1,128)S(1)} %all-gather.1.gain_ref, ...), custom_call_target="tpu_custom_call" | custom-call | tf_op jit(solution)/shard_map/stage_forward/pallas_call | solution.py:226
  160.7 11.6 %stage_forward.6 = (bf16[32,2048]{1,0:T(8,128)(2,1)S(1)}, bf16[4,32,2048]{2,1,0:T(8,128)(2,1)}, bf16[4,32,2048]{2,1,0:T(8,128)(2,1)}, bf16[4,32,1024]{2,1,0:T(8,128)(2,1)}, f32[4,32,512]{2,1,0:T(8,128)}) custom-call(bf16[32,2048]{1,0:T(8,128)(2,1)S(1)} %broadcast_select_fusion.8.x_ref, f32[4,1,2048]{2,1,0:T(1,128)S(1)} %all-gather.1.gain_ref, ...), custom_call_target="tpu_custom_call" | custom-call | tf_op jit(solution)/shard_map/stage_forward/pallas_call | solution.py:226
  173.7 11.6 %stage_forward.7 = (bf16[32,2048]{1,0:T(8,128)(2,1)}, bf16[4,32,2048]{2,1,0:T(8,128)(2,1)S(1)}, bf16[4,32,2048]{2,1,0:T(8,128)(2,1)S(1)}, bf16[4,32,1024]{2,1,0:T(8,128)(2,1)S(1)}, f32[4,32,512]{2,1,0:T(8,128)S(1)}) custom-call(bf16[32,2048]{1,0:T(8,128)(2,1)S(1)} %broadcast_select_fusion.9.x_ref, f32[4,1,2048]{2,1,0:T(1,128)S(1)} %all-gather.1.gain_ref, ...), custom_call_target="tpu_custom_call" | custom-call | tf_op jit(solution)/shard_map/stage_forward/pallas_call | solution.py:226
  185.3 11.7 %all_to_all.33 = bf16[4,32,2048]{2,1,0:T(8,128)(2,1)} all-to-all(bf16[4,32,2048]{2,1,0:T(8,128)(2,1)S(1)} %get-tuple-element.18.h_ref), channel_id=1, replica_groups=mesh['x'=4,'zl'=2,'c'=2,'y'=8,'zh'=4] {'zl','c'}, dimensions={0} | all-to-all | bytes 1048576 | tf_op jit(solution)/shard_map/all_to_all | solution.py:261
  201.8 13.6 %stage_backward.4 = (bf16[32,2048]{1,0:T(8,128)(2,1)S(1)}, bf16[4,32,1024]{2,1,0:T(8,128)(2,1)}) custom-call(bf16[32,2048]{1,0:T(8,128)(2,1)S(1)} %copy-done.10, f32[4,1,2048]{2,1,0:T(1,128)S(1)} %all-gather.1.gain_ref, bf16[4,32,2048]{2,1,0:T(8,128)(2,1)S(1)} %copy-done.5, bf16[4,32,2048]{2,1,0:T(8,128)(2,1)S(1)} %copy-done.2, ...), custom_call_target="tpu_custom_call" | custom-call | tf_op jit(solution)/shard_map/stage_backward/pallas_call | solution.py:246
  216.2 13.9 %stage_backward.5 = (bf16[32,2048]{1,0:T(8,128)(2,1)S(1)}, bf16[4,32,1024]{2,1,0:T(8,128)(2,1)}) custom-call(bf16[32,2048]{1,0:T(8,128)(2,1)S(1)} %broadcast_select_fusion.7.dy_ref, f32[4,1,2048]{2,1,0:T(1,128)S(1)} %all-gather.1.gain_ref, bf16[4,32,2048]{2,1,0:T(8,128)(2,1)S(1)} %copy-done.5, bf16[4,32,2048]{2,1,0:T(8,128)(2,1)S(1)} %copy-done.2, ...), custom_call_target="tpu_custom_call" | custom-call | tf_op jit(solution)/shard_map/stage_backward/pallas_call | solution.py:246
  230.8 14.5 %stage_backward.6 = (bf16[32,2048]{1,0:T(8,128)(2,1)}, bf16[4,32,1024]{2,1,0:T(8,128)(2,1)}) custom-call(bf16[32,2048]{1,0:T(8,128)(2,1)S(1)} %broadcast_select_fusion.5.dy_ref, f32[4,1,2048]{2,1,0:T(1,128)S(1)} %all-gather.1.gain_ref, bf16[4,32,2048]{2,1,0:T(8,128)(2,1)S(1)} %copy-done.5, bf16[4,32,2048]{2,1,0:T(8,128)(2,1)S(1)} %copy-done.2, ...), custom_call_target="tpu_custom_call" | custom-call | tf_op jit(solution)/shard_map/stage_backward/pallas_call | solution.py:246
  246.5 24.3 %collective-permute-done.23 = bf16[32,2048]{1,0:T(8,128)(2,1)} collective-permute-done((bf16[32,2048]{1,0:T(8,128)(2,1)}, bf16[32,2048]{1,0:T(8,128)(2,1)}, u32[]{:S(2)}, u32[]{:S(2)}) %collective-permute-start.23) | collective-permute-done | bytes 131104 | tf_op jit(solution)/shard_map/ppermute | solution.py:301
  274.8 14.3 %stage_backward.7 = (bf16[32,2048]{1,0:T(8,128)(2,1)}, bf16[4,32,1024]{2,1,0:T(8,128)(2,1)S(1)}) custom-call(bf16[32,2048]{1,0:T(8,128)(2,1)S(1)} %broadcast_select_fusion.2.dy_ref, f32[4,1,2048]{2,1,0:T(1,128)S(1)} %all-gather.1.gain_ref, bf16[4,32,2048]{2,1,0:T(8,128)(2,1)S(1)} %copy-done.6, bf16[4,32,2048]{2,1,0:T(8,128)(2,1)S(1)} %copy-done.3, ...), custom_call_target="tpu_custom_call" | custom-call | tf_op jit(solution)/shard_map/stage_backward/pallas_call | solution.py:246
  289.1 22.8 %all_to_all.34 = bf16[32,32,128]{2,1,0:T(8,128)(2,1)S(1)} all-to-all(bf16[32,32,128]{2,1,0:T(8,128)(2,1)S(1)} %bitcast.65), channel_id=1, replica_groups=mesh['x'=4,'zl'=2,'c'=2,'y'=8,'zh'=4] {'zl','c','y'}, dimensions={0} | all-to-all | bytes 524288 | tf_op jit(solution)/shard_map/all_to_all | solution.py:261
  312.0 3.6 convolution_convert_fusion
  315.6 26.5 %all_to_all.35 = bf16[32,64,128]{2,1,0:T(8,128)(2,1)S(1)} all-to-all(bf16[32,64,128]{2,1,0:T(8,128)(2,1)S(1)} %bitcast.67), channel_id=1, replica_groups=mesh['x'=4,'zl'=2,'c'=2,'y'=8,'zh'=4] {'y','zh'}, dimensions={0} | all-to-all | bytes 1048576 | tf_op jit(solution)/shard_map/all_to_all | solution.py:261
  343.5 17.3 %all_to_all.36 = f32[32,1,128]{2,1,0:T(1,128)S(1)} all-to-all(f32[32,1,128]{2,1,0:T(1,128)S(1)} %broadcast_in_dim.6), channel_id=1, replica_groups=mesh['x'=4,'zl'=2,'c'=2,'y'=8,'zh'=4] {'y','zh'}, dimensions={0} | all-to-all | bytes 32768 | tf_op jit(solution)/shard_map/all_to_all | solution.py:261
  362.0 10.5 %all_to_all.37 = f32[16,1,128]{2,1,0:T(1,128)S(1)} all-to-all(f32[16,1,128]{2,1,0:T(1,128)S(1)} %broadcast_in_dim.7), channel_id=1, replica_groups=mesh['x'=4,'zl'=2,'c'=2,'y'=8,'zh'=4] {'x','zl','c'}, dimensions={0} | all-to-all | bytes 16384 | tf_op jit(solution)/shard_map/all_to_all | solution.py:261
  377.8 2.7 collective-permute-done.24
  (107 shorter events, 49.9 us)
Async XLA Ops:
  7.2 116.3 %copy-start = (s32[4,32]{1,0:T(4,128)S(1)}, s32[4,32]{1,0:T(4,128)}, u32[]{:S(2)}) copy-start(s32[4,32]{1,0:T(4,128)} %param.9) | copy-start | bytes 1540
  7.2 304.8 %all-gather.4.cloned.1.call-start = ((), (), s32[]{:S(2)}) async-start(), calls=%async_computation.5 | async-start | bytes 4718592 | tf_op jit(solution)/shard_map/all_gather | solution.py:294
  8.2 10.7 %collective-permute-start = (bf16[1,64,1024]{2,1,0:T(8,128)(2,1)S(1)}, bf16[1,64,1024]{2,1,0:T(8,128)(2,1)S(1)}, u32[]{:S(2)}, u32[]{:S(2)}) collective-permute-start(bf16[1,64,1024]{2,1,0:T(8,128)(2,1)S(1)} %convert_element_type.24), channel_id=1, source_target_pairs={{0,2},{1,3},{2,0},{3,1},{4,6},{5,7},{6,4},{7,5},{8,10},{9,11},{10,... | collective-permute-start | bytes 393224 | tf_op jit(solution)/shard_map/ppermute | solution.py:72
  19.9 103.7 %copy-start.18 = (f32[1,2048]{1,0:T(1,128)S(1)}, f32[1,2048]{1,0:T(1,128)}, u32[]{:S(2)}) copy-start(f32[1,2048]{1,0:T(1,128)} %param.10) | copy-start | bytes 24580
  20.0 11.7 %collective-permute-start.1 = (bf16[2,64,1024]{2,1,0:T(8,128)(2,1)S(1)}, bf16[2,64,1024]{2,1,0:T(8,128)(2,1)S(1)}, u32[]{:S(2)}, u32[]{:S(2)}) collective-permute-start(bf16[2,64,1024]{2,1,0:T(8,128)(2,1)S(1)} %pad_maximum_fusion.2), channel_id=1, source_target_pairs={{0,1},{1,0},{2,3},{3,2},{4,5},{5,4},{6,7},{7,6},{8,9},{9,8},{10,11... | collective-permute-start | bytes 786440 | tf_op jit(solution)/shard_map/ppermute | solution.py:72
  31.8 9.9 %collective-permute-start.2 = (bf16[4,64,1024]{2,1,0:T(8,128)(2,1)S(1)}, bf16[4,64,1024]{2,1,0:T(8,128)(2,1)S(1)}, u32[]{:S(2)}, u32[]{:S(2)}) collective-permute-start(bf16[4,64,1024]{2,1,0:T(8,128)(2,1)S(1)} %bitcast.63), channel_id=1, source_target_pairs={{0,64},{1,65},{2,66},{3,67},{4,68},{5,69},{6,70},{7,71},{8,72},{9,... | collective-permute-start | bytes 1572872 | tf_op jit(solution)/shard_map/ppermute | solution.py:72
  42.0 23.9 %collective-permute-start.3 = (bf16[8,64,1024]{2,1,0:T(8,128)(2,1)S(1)}, bf16[8,64,1024]{2,1,0:T(8,128)(2,1)S(1)}, u32[]{:S(2)}, u32[]{:S(2)}) collective-permute-start(bf16[8,64,1024]{2,1,0:T(8,128)(2,1)S(1)} %pad_maximum_fusion.rest_0_), channel_id=1, source_target_pairs={{0,4},{1,5},{2,6},{3,7},{4,8},{5,9},{6,10},{7,11},{8,12},{9,13},{1... | collective-permute-start | bytes 3145736 | tf_op jit(solution)/shard_map/ppermute | solution.py:81
  46.5 21.2 %collective-permute-start.4 = (bf16[8,64,1024]{2,1,0:T(8,128)(2,1)S(1)}, bf16[8,64,1024]{2,1,0:T(8,128)(2,1)S(1)}, u32[]{:S(2)}, u32[]{:S(2)}) collective-permute-start(bf16[8,64,1024]{2,1,0:T(8,128)(2,1)S(1)} %pad_maximum_fusion.rest_0_), channel_id=1, source_target_pairs={{0,28},{1,29},{2,30},{3,31},{4,0},{5,1},{6,2},{7,3},{8,4},{9,5},{1... | collective-permute-start | bytes 3145736 | tf_op jit(solution)/shard_map/ppermute | solution.py:84
  65.9 17.1 %collective-permute-start.5 = (bf16[8,64,1024]{2,1,0:T(8,128)(2,1)S(1)}, bf16[8,64,1024]{2,1,0:T(8,128)(2,1)}, u32[]{:S(2)}, u32[]{:S(2)}) collective-permute-start(bf16[8,64,1024]{2,1,0:T(8,128)(2,1)S(1)} %collective-permute-done.3.rest_1_), channel_id=1, source_target_pairs={{0,4},{1,5},{2,6},{3,7},{4,8},{5,9},{6,10},{7,11},{8,12},{9,13},{1... | collective-permute-start | bytes 3145736 | tf_op jit(solution)/shard_map/ppermute | solution.py:81
  67.8 25.5 %collective-permute-start.6 = (bf16[8,64,1024]{2,1,0:T(8,128)(2,1)S(1)}, bf16[8,64,1024]{2,1,0:T(8,128)(2,1)}, u32[]{:S(2)}, u32[]{:S(2)}) collective-permute-start(bf16[8,64,1024]{2,1,0:T(8,128)(2,1)S(1)} %collective-permute-done.4.rest_2_), channel_id=1, source_target_pairs={{0,28},{1,29},{2,30},{3,31},{4,0},{5,1},{6,2},{7,3},{8,4},{9,5},{1... | collective-permute-start | bytes 3145736 | tf_op jit(solution)/shard_map/ppermute | solution.py:84
  83.0 17.4 %collective-permute-start.7 = (bf16[8,64,1024]{2,1,0:T(8,128)(2,1)}, bf16[8,64,1024]{2,1,0:T(8,128)(2,1)}, u32[]{:S(2)}, u32[]{:S(2)}) collective-permute-start(bf16[8,64,1024]{2,1,0:T(8,128)(2,1)} %collective-permute-done.5.rest_3_), channel_id=1, source_target_pairs={{0,4},{1,5},{2,6},{3,7},{4,8},{5,9},{6,10},{7,11},{8,12},{9,13},{1... | collective-permute-start | bytes 3145736 | tf_op jit(solution)/shard_map/ppermute | solution.py:81
  84.9 17.4 %collective-permute-start.10 = (bf16[8,64,1024]{2,1,0:T(8,128)(2,1)S(1)}, bf16[8,64,1024]{2,1,0:T(8,128)(2,1)S(1)}, u32[]{:S(2)}, u32[]{:S(2)}) collective-permute-start(bf16[8,64,1024]{2,1,0:T(8,128)(2,1)S(1)} %pad_maximum_fusion.rest_0_), channel_id=1, source_target_pairs={{0,32},{32,0},{1,33},{33,1},{2,34},{34,2},{3,35},{35,3},{4,36},{36... | collective-permute-start | bytes 3145736 | tf_op jit(solution)/shard_map/ppermute | solution.py:86
  88.9 18.2 %collective-permute-start.11 = (bf16[8,64,1024]{2,1,0:T(8,128)(2,1)S(1)}, bf16[8,64,1024]{2,1,0:T(8,128)(2,1)S(1)}, u32[]{:S(2)}, u32[]{:S(2)}) collective-permute-start(bf16[8,64,1024]{2,1,0:T(8,128)(2,1)S(1)} %collective-permute-done.3.rest_1_), channel_id=1, source_target_pairs={{0,32},{32,0},{1,33},{33,1},{2,34},{34,2},{3,35},{35,3},{4,36},{36... | collective-permute-start | bytes 3145736 | tf_op jit(solution)/shard_map/ppermute | solution.py:86
  90.9 18.3 %collective-permute-start.12 = (bf16[8,64,1024]{2,1,0:T(8,128)(2,1)S(1)}, bf16[8,64,1024]{2,1,0:T(8,128)(2,1)S(1)}, u32[]{:S(2)}, u32[]{:S(2)}) collective-permute-start(bf16[8,64,1024]{2,1,0:T(8,128)(2,1)S(1)} %collective-permute-done.4.rest_2_), channel_id=1, source_target_pairs={{0,32},{32,0},{1,33},{33,1},{2,34},{34,2},{3,35},{35,3},{4,36},{36... | collective-permute-start | bytes 3145736 | tf_op jit(solution)/shard_map/ppermute | solution.py:86
  93.3 18.7 %collective-permute-start.8 = (bf16[8,64,1024]{2,1,0:T(8,128)(2,1)}, bf16[8,64,1024]{2,1,0:T(8,128)(2,1)}, u32[]{:S(2)}, u32[]{:S(2)}) collective-permute-start(bf16[8,64,1024]{2,1,0:T(8,128)(2,1)} %collective-permute-done.6.rest_4_), channel_id=1, source_target_pairs={{0,28},{1,29},{2,30},{3,31},{4,0},{5,1},{6,2},{7,3},{8,4},{9,5},{1... | collective-permute-start | bytes 3145736 | tf_op jit(solution)/shard_map/ppermute | solution.py:84
  100.4 17.4 %collective-permute-start.9 = (bf16[8,64,1024]{2,1,0:T(8,128)(2,1)}, bf16[8,64,1024]{2,1,0:T(8,128)(2,1)}, u32[]{:S(2)}, u32[]{:S(2)}) collective-permute-start(bf16[8,64,1024]{2,1,0:T(8,128)(2,1)} %collective-permute-done.7.rest_5_), channel_id=1, source_target_pairs={{0,4},{1,5},{2,6},{3,7},{4,8},{5,9},{6,10},{7,11},{8,12},{9,13},{1... | collective-permute-start | bytes 3145736 | tf_op jit(solution)/shard_map/ppermute | solution.py:81
  102.3 28.0 %collective-permute-start.13 = (bf16[8,64,1024]{2,1,0:T(8,128)(2,1)}, bf16[8,64,1024]{2,1,0:T(8,128)(2,1)}, u32[]{:S(2)}, u32[]{:S(2)}) collective-permute-start(bf16[8,64,1024]{2,1,0:T(8,128)(2,1)} %collective-permute-done.5.rest_3_), channel_id=1, source_target_pairs={{0,32},{32,0},{1,33},{33,1},{2,34},{34,2},{3,35},{35,3},{4,36},{36... | collective-permute-start | bytes 3145736 | tf_op jit(solution)/shard_map/ppermute | solution.py:86
  107.2 23.1 %collective-permute-start.14 = (bf16[8,64,1024]{2,1,0:T(8,128)(2,1)}, bf16[8,64,1024]{2,1,0:T(8,128)(2,1)}, u32[]{:S(2)}, u32[]{:S(2)}) collective-permute-start(bf16[8,64,1024]{2,1,0:T(8,128)(2,1)} %collective-permute-done.6.rest_4_), channel_id=1, source_target_pairs={{0,32},{32,0},{1,33},{33,1},{2,34},{34,2},{3,35},{35,3},{4,36},{36... | collective-permute-start | bytes 3145736 | tf_op jit(solution)/shard_map/ppermute | solution.py:86
  109.2 21.2 %collective-permute-start.15 = (bf16[8,64,1024]{2,1,0:T(8,128)(2,1)}, bf16[8,64,1024]{2,1,0:T(8,128)(2,1)}, u32[]{:S(2)}, u32[]{:S(2)}) collective-permute-start(bf16[8,64,1024]{2,1,0:T(8,128)(2,1)} %collective-permute-done.7.rest_5_), channel_id=1, source_target_pairs={{0,32},{32,0},{1,33},{33,1},{2,34},{34,2},{3,35},{35,3},{4,36},{36... | collective-permute-start | bytes 3145736 | tf_op jit(solution)/shard_map/ppermute | solution.py:86
  112.0 18.3 %collective-permute-start.16 = (bf16[8,64,1024]{2,1,0:T(8,128)(2,1)}, bf16[8,64,1024]{2,1,0:T(8,128)(2,1)}, u32[]{:S(2)}, u32[]{:S(2)}) collective-permute-start(bf16[8,64,1024]{2,1,0:T(8,128)(2,1)} %collective-permute-done.8.rest_6_), channel_id=1, source_target_pairs={{0,32},{32,0},{1,33},{33,1},{2,34},{34,2},{3,35},{35,3},{4,36},{36... | collective-permute-start | bytes 3145736 | tf_op jit(solution)/shard_map/ppermute | solution.py:86
  117.7 12.6 %collective-permute-start.17 = (bf16[8,64,1024]{2,1,0:T(8,128)(2,1)}, bf16[8,64,1024]{2,1,0:T(8,128)(2,1)}, u32[]{:S(2)}, u32[]{:S(2)}) collective-permute-start(bf16[8,64,1024]{2,1,0:T(8,128)(2,1)} %collective-permute-done.9.rest_7_), channel_id=1, source_target_pairs={{0,32},{32,0},{1,33},{33,1},{2,34},{34,2},{3,35},{35,3},{4,36},{36... | collective-permute-start | bytes 3145736 | tf_op jit(solution)/shard_map/ppermute | solution.py:86
  141.9 5.9 %collective-permute-start.18 = (bf16[32,2048]{1,0:T(8,128)(2,1)S(1)}, bf16[32,2048]{1,0:T(8,128)(2,1)}, u32[]{:S(2)}, u32[]{:S(2)}) collective-permute-start(bf16[32,2048]{1,0:T(8,128)(2,1)S(1)} %get-tuple-element.15), channel_id=1, source_target_pairs={{0,128},{1,129},{2,130},{3,131},{4,132},{5,133},{6,134},{7,135},{8... | collective-permute-start | bytes 393224 | tf_op jit(solution)/shard_map/ppermute | solution.py:290
  159.4 1.3 collective-permute-start.19
  172.3 1.3 collective-permute-start.20
  215.4 0.7 collective-permute-start.21
  230.0 0.7 collective-permute-start.22
  230.7 14.5 %copy-start.11 = (bf16[32,2048]{1,0:T(8,128)(2,1)}, bf16[32,2048]{1,0:T(8,128)(2,1)S(1)}, u32[]{:S(2)}) copy-start(bf16[32,2048]{1,0:T(8,128)(2,1)S(1)} %broadcast_select_fusion.5.dy_ref) | copy-start | bytes 393220
  245.2 25.6 %collective-permute-start.23 = (bf16[32,2048]{1,0:T(8,128)(2,1)}, bf16[32,2048]{1,0:T(8,128)(2,1)}, u32[]{:S(2)}, u32[]{:S(2)}) collective-permute-start(bf16[32,2048]{1,0:T(8,128)(2,1)} %get-tuple-element.24), channel_id=1, source_target_pairs={{128,0},{129,1},{130,2},{131,3},{132,4},{133,5},{134,6},{135,7},{1... | collective-permute-start | bytes 393224 | tf_op jit(solution)/shard_map/ppermute | solution.py:301
  312.0 62.0 %copy-start.15 = (f32[1,64,1024]{2,1,0:T(8,128)S(1)}, f32[1,64,1024]{2,1,0:T(8,128)}, u32[]{:S(2)}) copy-start(f32[1,64,1024]{2,1,0:T(8,128)} %param.11) | copy-start | bytes 786436
  312.0 62.0 %copy-start.16 = (f32[1,64,1024]{2,1,0:T(8,128)S(1)}, f32[1,64,1024]{2,1,0:T(8,128)}, u32[]{:S(2)}) copy-start(f32[1,64,1024]{2,1,0:T(8,128)} %param.12) | copy-start | bytes 786436
  312.0 62.0 %copy-start.17 = (f32[1,64,1024]{2,1,0:T(8,128)S(1)}, f32[1,64,1024]{2,1,0:T(8,128)}, u32[]{:S(2)}) copy-start(f32[1,64,1024]{2,1,0:T(8,128)} %param.13) | copy-start | bytes 786436
  374.2 6.3 %collective-permute-start.24 = (bf16[64,1024]{1,0:T(8,128)(2,1)S(1)}, bf16[64,1024]{1,0:T(8,128)(2,1)S(1)}, u32[]{:S(2)}, u32[]{:S(2)}) collective-permute-start(bf16[64,1024]{1,0:T(8,128)(2,1)S(1)} %fusion.8), channel_id=1, source_target_pairs={{32,0},{64,32},{96,64},{128,96},{160,128},{192,160},{224,192},{256... | collective-permute-start | bytes 393224 | tf_op jit(solution)/shard_map/ppermute | solution.py:324
  (13 other events, 45.3 us)
Sparse Core Ops, SparseCore 0:
  198.0 69.9 all-gather.3

commit v2 on v1

v2 whole, which is shorter than its diff:
```python
import functools

import jax
import jax.numpy as jnp
from jax import lax
from jax.experimental import pallas as pl
from jax.experimental.pallas import tpu as pltpu
from jax.sharding import Mesh
from jax.sharding import PartitionSpec as P

HEAD = 128
X, ZL, C, Y, ZH = 4, 2, 2, 8, 4
AXES = ("x", "zl", "c", "y", "zh")
SECTION = ("x", "zl", "c")
DP = ("y", "zh")
LAYERS = ZL * C
RING = 8
PIECES = RING + 1
OFFSETS = (0, 1, -1, 2, -2, 3, -3, 4)
KV_HEADS = 4
GROUPS = 4
F32 = jnp.float32
BF16 = jnp.bfloat16


def flat(x, zl, c, y, zh):
    return (((x * ZL + zl) * C + c) * Y + y) * ZH + zh


def everywhere(target):
    pairs = []
    for x in range(X):
        for zl in range(ZL):
            for c in range(C):
                for y in range(Y):
                    for zh in range(ZH):
                        pairs.append((flat(x, zl, c, y, zh), flat(*target(x, zl, c, y, zh))))
    return pairs


def swap_route(bit):
    def target(x, zl, c, y, zh):
        if c == 1:
            return (x, zl, c, y ^ (1 << bit), zh)
        if bit == 0:
            return (x, zl ^ 1, c, y, zh)
        return (x, zl, c, y, zh ^ (1 << (bit - 1)))

    return everywhere(target)


def ring_route(step):
    def target(x, zl, c, y, zh):
        if c == 0:
            return (x, zl, c, (y + step) % Y, zh)
        z = (2 * zh + zl + step) % (ZL * ZH)
        return (x, z % 2, c, y, z // 2)

    return everywhere(target)


def gathered_weights(own, beside):
    c, y = lax.axis_index("c"), lax.axis_index("y")
    zl, zh = lax.axis_index("zl"), lax.axis_index("zh")
    rows, cols = own.shape
    bits = (
        jnp.where(c == 1, y // 4, zh // 2),
        jnp.where(c == 1, (y // 2) % 2, zh % 2),
        jnp.where(c == 1, y % 2, zl),
    )
    piece = own[None]
    for bit, mine, axis in ((2, bits[0], 0), (1, bits[1], 1), (0, bits[2], 0)):
        other = lax.ppermute(piece, AXES, swap_route(bit))
        low, high = jnp.where(mine == 0, piece, other), jnp.where(mine == 0, other, piece)
        if axis == 0:
            piece = jnp.concatenate([low, high], axis=0)
        else:
            piece = jnp.stack([low, high], axis=1).reshape(-1, rows, cols)
    pieces = [piece]
    up = down = piece
    for step in range(1, 4):
        if step == 2:
            up, down, ready = lax.optimization_barrier((up, down, beside(piece)))
        up = lax.ppermute(up, AXES, ring_route(1))
        down = lax.ppermute(down, AXES, ring_route(-1))
        pieces += [up, down]
    pieces.append(lax.ppermute(up[:4], AXES, ring_route(1)))
    pieces.append(lax.ppermute(down[4:], AXES, ring_route(-1)))
    others = [lax.ppermute(p, "c", [(0, 1), (1, 0)]) for p in pieces]
    return pieces + others, ready


def half(pieces, index, low):
    if index == RING - 1:
        return pieces[index + low]
    return pieces[index].at[pl.ds(4 * low, 4)]


def fetch_weights(pieces, w, sems, order):
    c, y = lax.axis_index("c"), lax.axis_index("y")
    zl = lax.axis_index("zl")
    z = 2 * lax.axis_index("zh") + zl

    def start(first, second, parity):
        for layer in order:
            for i, offset in enumerate(OFFSETS):
                if layer % 2 == 0:
                    there = lax.rem(y - offset + 2 * RING, RING)
                    pltpu.make_async_copy(
                        half(first, i, layer // 2),
                        w.at[layer, there // 2, lax.rem(there, 2)],
                        sems.at[layer],
                    ).start()
                elif (parity + offset) % 2 == layer // 2:
                    there = lax.rem(z - offset + 2 * RING, RING)
                    for low in range(2):
                        pltpu.make_async_copy(
                            half(second, i, low),
                            w.at[layer, :, low, there // 2],
                            sems.at[layer],
                        ).start()

    for core in range(C):
        for parity in range(ZL):

            @pl.when((c == core) & (zl == parity))
            def _():
                mine, others = pieces[:PIECES], pieces[PIECES:]
                first, second = (mine, others) if core == 0 else (others, mine)
                start(first, second, parity)


def wait_weights(w, sems, layer):
    pltpu.make_async_copy(w.at[layer], w.at[layer], sems.at[layer]).wait()


def head(block, index):
    return block[:, index * HEAD : (index + 1) * HEAD]


def stacked(block, group):
    return jnp.concatenate([head(block, group * GROUPS + a) for a in range(GROUPS)], axis=0)


def unstacked(blocks, length):
    return jnp.concatenate(
        [o[a * length : (a + 1) * length] for o in blocks for a in range(GROUPS)], axis=1
    )


def matmul(a, b, dims):
    return lax.dot_general(a, b, (dims, ((), ())), preferred_element_type=F32)


def forward_kernel(x_ref, gain_ref, mask_ref, *rest):
    w, y_ref, xs_ref, h_ref, kv_ref, p_ref = rest
    length, width = x_ref.shape
    y_ref[...] = x_ref[...]

    @pl.loop(0, LAYERS)
    def _(layer):
        x = y_ref[...]
        xs_ref[layer] = x
        xf = x.astype(F32)
        scale = lax.rsqrt(jnp.mean(xf * xf, axis=-1, keepdims=True) + 1e-05)
        h = (xf * scale * gain_ref[layer]).astype(BF16)
        h_ref[layer] = h
        whole = w[layer].reshape(width, -1)
        kv = matmul(h, whole, ((1,), (0,))).astype(BF16)
        kv_ref[layer] = kv
        groups = range(KV_HEADS)
        s = [matmul(head(kv, g), stacked(h, g), ((1,), (1,))) for g in groups]
        s = jnp.concatenate(s, axis=1)
        s = jnp.where(mask_ref[...] > 0, s * HEAD ** (-0.5), -1e30)
        e = jnp.exp(s - jnp.max(s, axis=0, keepdims=True))
        p = e / jnp.sum(e, axis=0, keepdims=True)
        p_ref[layer] = p
        pb = p.astype(BF16)
        o = [matmul(head(pb, g), head(kv, KV_HEADS + g), ((0,), (0,))) for g in groups]
        y_ref[...] = (xf + unstacked(o, length)).astype(BF16)


def backward_kernel(dy_ref, gain_ref, xs_ref, h_ref, kv_ref, p_ref, *rest):
    w, dx_ref, dkv_ref = rest
    length, width = dy_ref.shape
    dx_ref[...] = dy_ref[...]

    @pl.loop(0, LAYERS)
    def _(turn):
        layer = LAYERS - 1 - turn
        groups = range(KV_HEADS)
        dy, h, kv, p = dx_ref[...], h_ref[layer], kv_ref[layer], p_ref[layer]
        do = [stacked(dy, g) for g in groups]
        pb = p.astype(BF16)
        dv = [matmul(head(pb, g), do[g], ((1,), (0,))) for g in groups]
        dp = [matmul(head(kv, KV_HEADS + g), do[g], ((1,), (1,))) for g in groups]
        dp = jnp.concatenate(dp, axis=1)
        ds = p * (dp - jnp.sum(p * dp, axis=0, keepdims=True)) * HEAD ** (-0.5)
        ds = ds.astype(BF16)
        dk = [matmul(head(ds, g), stacked(h, g), ((1,), (0,))) for g in groups]
        dq = [matmul(head(ds, g), head(kv, g), ((0,), (0,))) for g in groups]
        dkv = jnp.concatenate(dk + dv, axis=1).astype(BF16)
        dkv_ref[layer] = dkv
        whole = w[layer].reshape(width, -1)
        dh = unstacked(dq, length) + matmul(dkv, whole, ((1,), (1,)))
        xf = xs_ref[layer].astype(F32)
        scale = lax.rsqrt(jnp.mean(xf * xf, axis=-1, keepdims=True) + 1e-05)
        gd = dh * gain_ref[layer]
        along = jnp.mean(xf * gd, axis=-1, keepdims=True) * (scale * scale * scale)
        dx_ref[...] = (dy.astype(F32) + (gd * scale - xf * along)).astype(BF16)


VMEM = pl.BlockSpec(memory_space=pltpu.VMEM)
ANY = pl.BlockSpec(memory_space=pl.ANY)
PARAMS = dict(vmem_limit_bytes=16 * 1024 * 1024)


def assemble_kernel(*refs):
    pieces, (w, sems) = refs[: 2 * PIECES], refs[2 * PIECES :]
    fetch_weights(pieces, w, sems, range(LAYERS))
    for layer in range(LAYERS):
        wait_weights(w, sems, layer)


def assembled(pieces):
    rows, columns = pieces[0].shape[1:]
    return pl.pallas_call(
        assemble_kernel,
        out_shape=pltpu.VMEM((LAYERS, Y // 2, 2, ZH, rows, columns), BF16),
        in_specs=[ANY] * (2 * PIECES),
        out_specs=VMEM,
        scratch_shapes=[pltpu.SemaphoreType.DMA((LAYERS,))],
        compiler_params=pltpu.CompilerParams(**PARAMS),
        name="assemble",
    )(*pieces)


def run_forward(x, gains, mask, w):
    length, width = x.shape
    columns = w.shape[-1]
    return pl.pallas_call(
        forward_kernel,
        out_shape=(
            jax.ShapeDtypeStruct((length, width), BF16),
            jax.ShapeDtypeStruct((LAYERS, length, width), BF16),
            jax.ShapeDtypeStruct((LAYERS, length, width), BF16),
            jax.ShapeDtypeStruct((LAYERS, length, columns), BF16),
            jax.ShapeDtypeStruct((LAYERS, length, KV_HEADS * HEAD), F32),
        ),
        in_specs=[VMEM] * 4,
        out_specs=(VMEM,) * 5,
        compiler_params=pltpu.CompilerParams(**PARAMS),
        name="stage_forward",
    )(x, gains, mask, w)


def run_backward(dy, gains, saved, w):
    length, width = dy.shape
    columns = w.shape[-1]
    return pl.pallas_call(
        backward_kernel,
        out_shape=(
            jax.ShapeDtypeStruct((length, width), BF16),
            jax.ShapeDtypeStruct((LAYERS, length, columns), BF16),
        ),
        in_specs=[VMEM] * 7,
        out_specs=(VMEM,) * 2,
        compiler_params=pltpu.CompilerParams(**PARAMS),
        name="stage_backward",
    )(dy, gains, *saved, w)


def exchange(block, axes):
    return lax.all_to_all(block, axes, split_axis=0, concat_axis=0, tiled=True)


def total_of(value):
    for axes, count in ((DP, Y * ZH), (SECTION, X * ZL * C)):
        sent = jnp.broadcast_to(value.reshape(1, 1), (count, 128))
        value = jnp.sum(exchange(sent, axes)[:, 0])
    return value


def body(inputs, upstream, segments, gains, master, moment, second):
    stage = lax.axis_index("x")
    which = lax.axis_index("zl") * C + lax.axis_index("c")
    length, width = inputs.shape[1:]
    rows, columns = master.shape[1:]

    def beside(piece):
        mine, _ = lax.optimization_barrier((gains, piece))
        plane_gains = lax.all_gather(mine, ("zl", "c"), axis=0)
        seg = lax.dynamic_index_in_dim(segments, which, 0, keepdims=False)
        place = jnp.arange(length)
        allowed = (place[None, :] >= place[:, None]) & (seg[None, :] == seg[:, None])
        mask = jnp.tile(allowed.astype(F32), (1, GROUPS * KV_HEADS))
        first = lax.dynamic_index_in_dim(inputs, which, 0, keepdims=False)
        last = lax.dynamic_index_in_dim(upstream, which, 0, keepdims=False)
        is_stage = tuple(stage == i for i in range(X))
        return plane_gains, mask, first, last, is_stage

    pieces, (plane_gains, mask, first, last, is_stage) = gathered_weights(master[0].astype(BF16), beside)
    w = assembled(pieces)

    held = first
    for turn in range(X):
        y, *saved = run_forward(held, plane_gains, mask, w)
        if turn < X - 1:
            arrived = lax.ppermute(y, "x", [(turn, turn + 1)])
            held = jnp.where(is_stage[turn + 1], arrived, held)
        if turn == X - 2:
            h, _ = lax.optimization_barrier((saved[1], arrived))
            early = lax.cond(
                is_stage[X - 1], lambda: jnp.zeros_like(h), lambda: exchange(h, ("zl", "c"))
            )

    held = last
    for turn in range(X):
        here = X - 1 - turn
        dx, dkv = run_backward(held, plane_gains, saved, w)
        if turn < X - 1:
            arrived = lax.ppermute(dx, "x", [(here, here - 1)])
            held = jnp.where(is_stage[here - 1], arrived, held)
        if turn == 0:
            h, _ = lax.optimization_barrier((saved[1], arrived))
            layer_h = lax.cond(
                is_stage[X - 1], lambda: exchange(h, ("zl", "c")), lambda: early
            )
            all_h = lax.all_gather(
                layer_h.reshape(LAYERS * length, width), "y", axis=0, tiled=True
            )

    sent = dkv.reshape(LAYERS, length, Y, columns // Y).transpose(0, 2, 1, 3)
    sent = sent.reshape(LAYERS * Y, length, columns // Y)
    got = exchange(sent, ("zl", "c", "y")).reshape(LAYERS, Y, length, columns // Y)
    tokens = got.transpose(1, 0, 2, 3).reshape(Y * LAYERS * length, columns // Y)
    partial = lax.dot_general(
        all_h, tokens, (((0,), (0,)), ((), ())), preferred_element_type=F32
    ).astype(BF16)
    got = exchange(partial.reshape(Y * ZH, rows, columns // Y), DP)
    grad = jnp.sum(got.reshape(Y, ZH, rows, columns // Y).astype(F32), axis=1)
    grad = grad.transpose(1, 0, 2).reshape(rows, columns)

    total = total_of(jnp.sum(grad * grad))
    entries = X * ZL * C * Y * ZH * grad.size
    factor = jnp.minimum(1.0, 0.01 / jnp.sqrt(total / entries))
    scaled = grad * factor
    new_moment = 0.9 * moment[0] + 0.1 * scaled
    new_second = 0.95 * second[0] + 0.05 * scaled * scaled
    new_master = master[0] - 0.002 * new_moment / (jnp.sqrt(new_second) + 1e-08)
    sections = X * ZL * C
    route = [((i + 1) % sections, i) for i in range(sections)]
    replica = lax.ppermute(new_master.astype(BF16), SECTION, route)
    return (new_master[None], new_moment[None], new_second[None], replica[None])


def solution(mesh):
    fine = Mesh(mesh.devices.reshape(X, ZL, C, Y, ZH), AXES)
    state = P(SECTION, DP, None)
    return jax.shard_map(
        body,
        mesh=fine,
        in_specs=(
            P(None, DP, None),
            P(None, DP, None),
            P(None, DP),
            P(SECTION, None),
            state,
            state,
            state,
        ),
        out_specs=(state,) * 4,
        check_vma=False,
    )
```

time: 389 us -> 336 us (0.86)
  Pallas kernels: 103 us -> 55.3 us
  waiting for transfers between devices: 71.6 us -> 60 us
    pallas_call x4, Pallas kernels: 56.2 us -> 30.9 us  [run_backward(): pl.pallas_call(backward_kernel, out_shape=(jax.ShapeDtypeStruct((length,...]
    pallas_call x4, Pallas kernels: 46.4 us -> 23.1 us  [run_forward(): pl.pallas_call(forward_kernel, out_shape=(jax.ShapeDtypeStruct((length, w...]
    ppermute x4 -> x3, waiting for transfers between devices: 25.4 us -> 13.7 us  [gathered_weights(): up = lax.ppermute(up, AXES, ring_route(1))]
    ppermute x0 -> x2, starting transfers between devices: none -> 8.59 us  [the longest x1 6.67 us: gathered_weights(): pieces.append(lax.ppermute(down[4:], AXES, ring_route(-1)))]
    ppermute x3, waiting for transfers between devices: 24.3 us -> 17.1 us  [body(): arrived = lax.ppermute(dx, 'x', [(here, here - 1)])]
    all_gather x1, waiting for transfers between devices: 0.02 us -> 4.44 us  [body(): lax.all_gather(layer_h.reshape(LAYERS * length, width), 'y', axis=0, tile...]
    ppermute x4 -> x3, starting transfers between devices: 10.3 us -> 8.41 us  [gathered_weights(): up = lax.ppermute(up, AXES, ring_route(1))]
    unnamed x39 -> x17, local copies, waits for them, and re-layouts: 8.48 us -> 7.25 us
  transfers between devices with their start and end apart: 26 -> 28, of which waited for: 11 -> 13; matrix products, arithmetic and copies ran while one was open for 1% -> 1% of each run, Pallas kernels for 14% -> 7%
where the time goes in v2:
time: 336 us; the launch traced here: 335 us
  blocking collectives  97.5 us (29%)
  starting transfers between devices  86.2 us (26%)
  waiting for transfers between devices  60 us (18%)
  Pallas kernels  55.3 us (16%)
  between operations  15.4 us (5%)
  local copies, waits for them, and re-layouts  11.7 us (3%)
  other arithmetic  5.63 us (2%)
  matrix products  3.58 us (1%)
    all_to_all x5, blocking collectives, exchange(): return lax.all_to_all(block, axes, split_axis=0, concat_axis=0, tiled=True)  91.5 us
    pallas_call x4, Pallas kernels, run_backward(): pl.pallas_call(backward_kernel, out_shape=(jax.ShapeDtypeStruct((length,...  30.9 us
    ppermute x9, starting transfers between devices, gathered_weights(): others = [lax.ppermute(p, 'c', [(0, 1), (1, 0)]) for p in pieces]  25.1 us
    pallas_call x4, Pallas kernels, run_forward(): pl.pallas_call(forward_kernel, out_shape=(jax.ShapeDtypeStruct((length, w...  23.1 us
    ppermute x3, starting transfers between devices, gathered_weights(): down = lax.ppermute(down, AXES, ring_route(-1))  18.7 us
    ppermute x3, waiting for transfers between devices, body(): arrived = lax.ppermute(dx, 'x', [(here, here - 1)])  17.1 us
    ppermute x3, waiting for transfers between devices, gathered_weights(): other = lax.ppermute(piece, AXES, swap_route(bit))  16.6 us
    ppermute x3, starting transfers between devices, gathered_weights(): other = lax.ppermute(piece, AXES, swap_route(bit))  15.6 us
  transfers between devices with their start and end apart: 28, of which 13 were waited for; matrix products, arithmetic and copies ran while one was open for 1% of the time, Pallas kernels for 7%

profile of v2, /device:TPU:1, one launch (start us, length us, event | category | flops | bytes accessed | tf_op | source)
XLA Modules:
  0.0 335.4 jit_solution(9938643806578210089)
XLA Ops:
  8.2 8.3 %collective-permute-start = (bf16[1,64,1024]{2,1,0:T(8,128)(2,1)S(1)}, bf16[1,64,1024]{2,1,0:T(8,128)(2,1)S(1)}, u32[]{:S(2)}, u32[]{:S(2)}) collective-permute-start(bf16[1,64,1024]{2,1,0:T(8,128)(2,1)S(1)} %convert_element_type.27), channel_id=1, source_target_pairs={{0,2},{1,3},{2,0},{3,1},{4,6},{5,7},{6,4},{7,5},{8,10},{9,11},{10,... | collective-permute-start | bytes 393224 | tf_op jit(solution)/shard_map/ppermute | solution.py:73
  19.9 5.4 %collective-permute-start.1 = (bf16[2,64,1024]{2,1,0:T(8,128)(2,1)S(1)}, bf16[2,64,1024]{2,1,0:T(8,128)(2,1)S(1)}, u32[]{:S(2)}, u32[]{:S(2)}) collective-permute-start(bf16[2,64,1024]{2,1,0:T(8,128)(2,1)S(1)} %pad_maximum_fusion.2), channel_id=1, source_target_pairs={{0,1},{1,0},{2,3},{3,2},{4,5},{5,4},{6,7},{7,6},{8,9},{9,8},{10,11... | collective-permute-start | bytes 786440 | tf_op jit(solution)/shard_map/ppermute | solution.py:73
  25.4 6.2 %collective-permute-done.1 = bf16[2,64,1024]{2,1,0:T(8,128)(2,1)S(1)} collective-permute-done((bf16[2,64,1024]{2,1,0:T(8,128)(2,1)S(1)}, bf16[2,64,1024]{2,1,0:T(8,128)(2,1)S(1)}, u32[]{:S(2)}, u32[]{:S(2)}) %collective-permute-start.1) | collective-permute-done | bytes 262176 | tf_op jit(solution)/shard_map/ppermute | solution.py:73
  33.7 8.0 %collective-permute-done.2 = bf16[4,64,1024]{2,1,0:T(8,128)(2,1)S(1)} collective-permute-done((bf16[4,64,1024]{2,1,0:T(8,128)(2,1)S(1)}, bf16[4,64,1024]{2,1,0:T(8,128)(2,1)S(1)}, u32[]{:S(2)}, u32[]{:S(2)}) %collective-permute-start.2) | collective-permute-done | bytes 524320 | tf_op jit(solution)/shard_map/ppermute | solution.py:73
  41.9 4.6 %collective-permute-start.3 = (bf16[8,64,1024]{2,1,0:T(8,128)(2,1)S(1)}, bf16[8,64,1024]{2,1,0:T(8,128)(2,1)S(1)}, u32[]{:S(2)}, u32[]{:S(2)}) collective-permute-start(bf16[8,64,1024]{2,1,0:T(8,128)(2,1)S(1)} %pad_maximum_fusion.refs_0_), channel_id=1, source_target_pairs={{0,4},{1,5},{2,6},{3,7},{4,8},{5,9},{6,10},{7,11},{8,12},{9,13},{1... | collective-permute-start | bytes 3145736 | tf_op jit(solution)/shard_map/ppermute | solution.py:84
  46.5 8.8 %collective-permute-start.4 = (bf16[8,64,1024]{2,1,0:T(8,128)(2,1)S(1)}, bf16[8,64,1024]{2,1,0:T(8,128)(2,1)S(1)}, u32[]{:S(2)}, u32[]{:S(2)}) collective-permute-start(bf16[8,64,1024]{2,1,0:T(8,128)(2,1)S(1)} %pad_maximum_fusion.refs_0_), channel_id=1, source_target_pairs={{0,28},{1,29},{2,30},{3,31},{4,0},{5,1},{6,2},{7,3},{8,4},{9,5},{1... | collective-permute-start | bytes 3145736 | tf_op jit(solution)/shard_map/ppermute | solution.py:85
  58.2 6.0 %all-gather.1.gain_ref = f32[4,1,2048]{2,1,0:T(1,128)S(1)} all-gather(f32[1,1,2048]{2,1,0:T(1,128)S(1)} %bitcast.72), channel_id=2, replica_groups=mesh['x'=4,'zl'=2,'c'=2,'y'=8,'zh'=4] {'zl','c'}, dimensions={0}, use_global_device_ids=true | all-gather | bytes 40960 | tf_op jit(solution)/shard_map/all_gather | solution.py:292
  69.0 5.3 %collective-permute-start.6 = (bf16[8,64,1024]{2,1,0:T(8,128)(2,1)S(1)}, bf16[8,64,1024]{2,1,0:T(8,128)(2,1)S(1)}, u32[]{:S(2)}, u32[]{:S(2)}) collective-permute-start(bf16[8,64,1024]{2,1,0:T(8,128)(2,1)S(1)} %collective-permute-done.4.refs_2_), channel_id=1, source_target_pairs={{0,28},{1,29},{2,30},{3,31},{4,0},{5,1},{6,2},{7,3},{8,4},{9,5},{1... | collective-permute-start | bytes 3145736 | tf_op jit(solution)/shard_map/ppermute | solution.py:85
  74.3 10.5 %collective-permute-done.5.refs_3_ = bf16[8,64,1024]{2,1,0:T(8,128)(2,1)S(1)} collective-permute-done((bf16[8,64,1024]{2,1,0:T(8,128)(2,1)S(1)}, bf16[8,64,1024]{2,1,0:T(8,128)(2,1)S(1)}, u32[]{:S(2)}, u32[]{:S(2)}) %collective-permute-start.5) | collective-permute-done | bytes 1048608 | tf_op jit(solution)/shard_map/ppermute | solution.py:84
  86.8 4.6 %collective-permute-start.8 = (bf16[8,64,1024]{2,1,0:T(8,128)(2,1)S(1)}, bf16[8,64,1024]{2,1,0:T(8,128)(2,1)S(1)}, u32[]{:S(2)}, u32[]{:S(2)}) collective-permute-start(bf16[8,64,1024]{2,1,0:T(8,128)(2,1)S(1)} %collective-permute-done.6.refs_4_), channel_id=1, source_target_pairs={{0,28},{1,29},{2,30},{3,31},{4,0},{5,1},{6,2},{7,3},{8,4},{9,5},{1... | collective-permute-start | bytes 3145736 | tf_op jit(solution)/shard_map/ppermute | solution.py:85
  91.3 4.7 %collective-permute-start.11 = (bf16[8,64,1024]{2,1,0:T(8,128)(2,1)S(1)}, bf16[8,64,1024]{2,1,0:T(8,128)(2,1)S(1)}, u32[]{:S(2)}, u32[]{:S(2)}) collective-permute-start(bf16[8,64,1024]{2,1,0:T(8,128)(2,1)S(1)} %pad_maximum_fusion.refs_0_), channel_id=1, source_target_pairs={{0,32},{32,0},{1,33},{33,1},{2,34},{34,2},{3,35},{35,3},{4,36},{36... | collective-permute-start | bytes 3145736 | tf_op jit(solution)/shard_map/ppermute | solution.py:89
  101.9 4.9 %collective-permute-start.14 = (bf16[8,64,1024]{2,1,0:T(8,128)(2,1)S(1)}, bf16[8,64,1024]{2,1,0:T(8,128)(2,1)S(1)}, u32[]{:S(2)}, u32[]{:S(2)}) collective-permute-start(bf16[8,64,1024]{2,1,0:T(8,128)(2,1)S(1)} %collective-permute-done.5.refs_3_), channel_id=1, source_target_pairs={{0,32},{32,0},{1,33},{33,1},{2,34},{34,2},{3,35},{35,3},{4,36},{36... | collective-permute-start | bytes 3145736 | tf_op jit(solution)/shard_map/ppermute | solution.py:89
  111.4 6.7 %collective-permute-start.10 = (bf16[4,64,1024]{2,1,0:T(8,128)(2,1)S(1)}, bf16[4,64,1024]{2,1,0:T(8,128)(2,1)S(1)}, u32[]{:S(2)}, u32[]{:S(2)}) collective-permute-start(bf16[4,64,1024]{2,1,0:T(8,128)(2,1)S(1)} %slice.17), channel_id=1, source_target_pairs={{0,28},{1,29},{2,30},{3,31},{4,0},{5,1},{6,2},{7,3},{8,4},{9,5},{1... | collective-permute-start | bytes 1572872 | tf_op jit(solution)/shard_map/ppermute | solution.py:88
  130.0 6.6 %stage_forward.4 = (bf16[32,2048]{1,0:T(8,128)(2,1)S(1)}, bf16[4,32,2048]{2,1,0:T(8,128)(2,1)}, bf16[4,32,2048]{2,1,0:T(8,128)(2,1)}, bf16[4,32,1024]{2,1,0:T(8,128)(2,1)}, f32[4,32,512]{2,1,0:T(8,128)}) custom-call(bf16[32,2048]{1,0:T(8,128)(2,1)S(1)} %get-tuple-element.42.x_ref, f32[4,1,2048]{2,1,0:T(1,128)S(1)} %all-gather.1.gain_ref, ...), custom_call_target="tpu_custom_call" | custom-call | tf_op jit(solution)/shard_map/stage_forward/pallas_call | solution.py:241
  136.6 3.1 collective-permute-start.20
  142.2 5.6 %stage_forward.5 = (bf16[32,2048]{1,0:T(8,128)(2,1)S(1)}, bf16[4,32,2048]{2,1,0:T(8,128)(2,1)}, bf16[4,32,2048]{2,1,0:T(8,128)(2,1)}, bf16[4,32,1024]{2,1,0:T(8,128)(2,1)}, f32[4,32,512]{2,1,0:T(8,128)}) custom-call(bf16[32,2048]{1,0:T(8,128)(2,1)S(1)} %broadcast_select_fusion.5.x_ref, f32[4,1,2048]{2,1,0:T(1,128)S(1)} %all-gather.1.gain_ref, ...), custom_call_target="tpu_custom_call" | custom-call | tf_op jit(solution)/shard_map/stage_forward/pallas_call | solution.py:241
  148.5 5.4 %stage_forward.6 = (bf16[32,2048]{1,0:T(8,128)(2,1)S(1)}, bf16[4,32,2048]{2,1,0:T(8,128)(2,1)}, bf16[4,32,2048]{2,1,0:T(8,128)(2,1)S(1)}, bf16[4,32,1024]{2,1,0:T(8,128)(2,1)}, f32[4,32,512]{2,1,0:T(8,128)}) custom-call(bf16[32,2048]{1,0:T(8,128)(2,1)S(1)} %broadcast_select_fusion.7.x_ref, f32[4,1,2048]{2,1,0:T(1,128)S(1)} %all-gather.1.gain_ref, ...), custom_call_target="tpu_custom_call" | custom-call | tf_op jit(solution)/shard_map/stage_forward/pallas_call | solution.py:241
  154.7 5.5 %stage_forward.7 = (bf16[32,2048]{1,0:T(8,128)(2,1)}, bf16[4,32,2048]{2,1,0:T(8,128)(2,1)S(1)}, bf16[4,32,2048]{2,1,0:T(8,128)(2,1)S(1)}, bf16[4,32,1024]{2,1,0:T(8,128)(2,1)S(1)}, f32[4,32,512]{2,1,0:T(8,128)S(1)}) custom-call(bf16[32,2048]{1,0:T(8,128)(2,1)S(1)} %broadcast_select_fusion.3.x_ref, f32[4,1,2048]{2,1,0:T(1,128)S(1)} %all-gather.1.gain_ref, ...), custom_call_target="tpu_custom_call" | custom-call | tf_op jit(solution)/shard_map/stage_forward/pallas_call | solution.py:241
  160.2 7.7 %stage_backward.4 = (bf16[32,2048]{1,0:T(8,128)(2,1)S(1)}, bf16[4,32,1024]{2,1,0:T(8,128)(2,1)}) custom-call(bf16[32,2048]{1,0:T(8,128)(2,1)S(1)} %get-tuple-element.53.dy_ref, f32[4,1,2048]{2,1,0:T(1,128)S(1)} %all-gather.1.gain_ref, bf16[4,32,2048]{2,1,0:T(8,128)(2,1)S(1)} %get-tuple-element.54.xs_ref, bf16[4,32,2048]{2,1,0:T(8,128)(2,1)S(1)} %get-tuple-element.58.h_ref, ...), custom_call_target="tpu_custom_call" | custom-call | tf_op jit(solution)/shard_map/stage_backward/pallas_call | solution.py:260
  168.6 11.4 %conditional.2 = (bf16[4,32,2048]{2,1,0:T(8,128)(2,1)S(1)}) conditional(s32[]{:T(128)} %convert_element_type.29, bf16[4,32,2048]{2,1,0:T(8,128)(2,1)S(1)} %get-tuple-element.51, () %tuple.27), branch_computations={%region_0.1_spmd, %region_1.2_spmd} | conditional | bytes 1048584 | solution.py:313
  168.6 11.4 %all_to_all.36 = bf16[4,32,2048]{2,1,0:T(8,128)(2,1)S(1)} all-to-all(bf16[4,32,2048]{2,1,0:T(8,128)(2,1)S(1)} %param), channel_id=1, replica_groups=mesh['x'=4,'zl'=2,'c'=2,'y'=8,'zh'=4] {'zl','c'}, dimensions={0} | all-to-all | bytes 1048576 | tf_op jit(solution)/shard_map/cond/branch_0_fun/all_to_all | solution.py:274
  180.9 5.8 %copy-done.2 = bf16[4,4,2,4,64,1024]{5,4,3,2,1,0:T(8,128)(2,1)S(1)} copy-done((bf16[4,4,2,4,64,1024]{5,4,3,2,1,0:T(8,128)(2,1)S(1)}, bf16[4,4,2,4,64,1024]{5,4,3,2,1,0:T(8,128)(2,1)}, u32[]{:S(2)}) %copy-start.2) | copy-done | bytes 16777240
  186.6 7.7 %stage_backward.5 = (bf16[32,2048]{1,0:T(8,128)(2,1)S(1)}, bf16[4,32,1024]{2,1,0:T(8,128)(2,1)}) custom-call(bf16[32,2048]{1,0:T(8,128)(2,1)S(1)} %broadcast_select_fusion.6.dy_ref, f32[4,1,2048]{2,1,0:T(1,128)S(1)} %all-gather.1.gain_ref, bf16[4,32,2048]{2,1,0:T(8,128)(2,1)S(1)} %get-tuple-element.54.xs_ref, ...), custom_call_target="tpu_custom_call" | custom-call | tf_op jit(solution)/shard_map/stage_backward/pallas_call | solution.py:260
  195.0 7.7 %stage_backward.6 = (bf16[32,2048]{1,0:T(8,128)(2,1)S(1)}, bf16[4,32,1024]{2,1,0:T(8,128)(2,1)}) custom-call(bf16[32,2048]{1,0:T(8,128)(2,1)S(1)} %broadcast_select_fusion.4.dy_ref, f32[4,1,2048]{2,1,0:T(1,128)S(1)} %all-gather.1.gain_ref, bf16[4,32,2048]{2,1,0:T(8,128)(2,1)S(1)} %get-tuple-element.54.xs_ref, ...), custom_call_target="tpu_custom_call" | custom-call | tf_op jit(solution)/shard_map/stage_backward/pallas_call | solution.py:260
  204.0 17.1 %collective-permute-done.25 = bf16[32,2048]{1,0:T(8,128)(2,1)S(1)} collective-permute-done((bf16[32,2048]{1,0:T(8,128)(2,1)S(1)}, bf16[32,2048]{1,0:T(8,128)(2,1)S(1)}, u32[]{:S(2)}, u32[]{:S(2)}) %collective-permute-start.25) | collective-permute-done | bytes 131104 | tf_op jit(solution)/shard_map/ppermute | solution.py:322
  221.2 7.8 %stage_backward.7 = (bf16[32,2048]{1,0:T(8,128)(2,1)}, bf16[4,32,1024]{2,1,0:T(8,128)(2,1)S(1)}) custom-call(bf16[32,2048]{1,0:T(8,128)(2,1)S(1)} %broadcast_select_fusion.2.dy_ref, f32[4,1,2048]{2,1,0:T(1,128)S(1)} %all-gather.1.gain_ref, bf16[4,32,2048]{2,1,0:T(8,128)(2,1)S(1)} %get-tuple-element.54.xs_ref, ...), custom_call_target="tpu_custom_call" | custom-call | tf_op jit(solution)/shard_map/stage_backward/pallas_call | solution.py:260
  229.0 23.1 %all_to_all.38 = bf16[32,32,128]{2,1,0:T(8,128)(2,1)S(1)} all-to-all(bf16[32,32,128]{2,1,0:T(8,128)(2,1)S(1)} %bitcast.65), channel_id=1, replica_groups=mesh['x'=4,'zl'=2,'c'=2,'y'=8,'zh'=4] {'zl','c','y'}, dimensions={0} | all-to-all | bytes 524288 | tf_op jit(solution)/shard_map/all_to_all | solution.py:274
  252.1 4.4 %all-gather.4.cloned.1.call-done = bf16[1024,2048]{1,0:T(8,128)(2,1)} async-done(((bf16[128,2048]{1,0:T(8,128)(2,1)}), bf16[1024,2048]{1,0:T(8,128)(2,1)}) %all-gather.4.cloned.1.call-update) | async-done | bytes 4194320 | tf_op jit(solution)/shard_map/all_gather | solution.py:329
  256.6 3.6 %convolution_convert_fusion = bf16[2048,128]{1,0:T(8,128)(2,1)S(1)} fusion(bf16[1024,2048]{1,0:T(8,128)(2,1)} %all-gather.4.cloned.1.call-done, bf16[1024,128]{1,0:T(8,128)(2,1)S(1)} %bitcast.68), kind=kOutput, calls=%fused_computation | convolution fusion | flops 537133056 | bytes 4980736 | tf_op jit(solution)/shard_map/dot_general | solution.py:337
  260.1 27.2 %all_to_all.39 = bf16[32,64,128]{2,1,0:T(8,128)(2,1)S(1)} all-to-all(bf16[32,64,128]{2,1,0:T(8,128)(2,1)S(1)} %bitcast.67), channel_id=1, replica_groups=mesh['x'=4,'zl'=2,'c'=2,'y'=8,'zh'=4] {'y','zh'}, dimensions={0} | all-to-all | bytes 1048576 | tf_op jit(solution)/shard_map/all_to_all | solution.py:274
  288.8 17.5 %all_to_all.40 = f32[32,1,128]{2,1,0:T(1,128)S(1)} all-to-all(f32[32,1,128]{2,1,0:T(1,128)S(1)} %broadcast_in_dim.6), channel_id=1, replica_groups=mesh['x'=4,'zl'=2,'c'=2,'y'=8,'zh'=4] {'y','zh'}, dimensions={0} | all-to-all | bytes 32768 | tf_op jit(solution)/shard_map/all_to_all | solution.py:274
  307.5 12.3 %all_to_all.41 = f32[16,1,128]{2,1,0:T(1,128)S(1)} all-to-all(f32[16,1,128]{2,1,0:T(1,128)S(1)} %broadcast_in_dim.7), channel_id=1, replica_groups=mesh['x'=4,'zl'=2,'c'=2,'y'=8,'zh'=4] {'x','zl','c'}, dimensions={0} | all-to-all | bytes 16384 | tf_op jit(solution)/shard_map/all_to_all | solution.py:274
  (94 shorter events, 56.5 us)
Async XLA Ops:
  7.2 48.2 %copy-start = (s32[4,32]{1,0:T(4,128)S(1)}, s32[4,32]{1,0:T(4,128)}, u32[]{:S(2)}) copy-start(s32[4,32]{1,0:T(4,128)} %param.13) | copy-start | bytes 1540
  7.2 249.4 %all-gather.4.cloned.1.call-start = ((), (), s32[]{:S(2)}) async-start(), calls=%async_computation.6 | async-start | bytes 4718592 | tf_op jit(solution)/shard_map/all_gather | solution.py:329
  8.2 10.7 %collective-permute-start = (bf16[1,64,1024]{2,1,0:T(8,128)(2,1)S(1)}, bf16[1,64,1024]{2,1,0:T(8,128)(2,1)S(1)}, u32[]{:S(2)}, u32[]{:S(2)}) collective-permute-start(bf16[1,64,1024]{2,1,0:T(8,128)(2,1)S(1)} %convert_element_type.27), channel_id=1, source_target_pairs={{0,2},{1,3},{2,0},{3,1},{4,6},{5,7},{6,4},{7,5},{8,10},{9,11},{10,... | collective-permute-start | bytes 393224 | tf_op jit(solution)/shard_map/ppermute | solution.py:73
  19.9 11.7 %collective-permute-start.1 = (bf16[2,64,1024]{2,1,0:T(8,128)(2,1)S(1)}, bf16[2,64,1024]{2,1,0:T(8,128)(2,1)S(1)}, u32[]{:S(2)}, u32[]{:S(2)}) collective-permute-start(bf16[2,64,1024]{2,1,0:T(8,128)(2,1)S(1)} %pad_maximum_fusion.2), channel_id=1, source_target_pairs={{0,1},{1,0},{2,3},{3,2},{4,5},{5,4},{6,7},{7,6},{8,9},{9,8},{10,11... | collective-permute-start | bytes 786440 | tf_op jit(solution)/shard_map/ppermute | solution.py:73
  31.7 9.9 %collective-permute-start.2 = (bf16[4,64,1024]{2,1,0:T(8,128)(2,1)S(1)}, bf16[4,64,1024]{2,1,0:T(8,128)(2,1)S(1)}, u32[]{:S(2)}, u32[]{:S(2)}) collective-permute-start(bf16[4,64,1024]{2,1,0:T(8,128)(2,1)S(1)} %bitcast.63), channel_id=1, source_target_pairs={{0,64},{1,65},{2,66},{3,67},{4,68},{5,69},{6,70},{7,71},{8,72},{9,... | collective-permute-start | bytes 1572872 | tf_op jit(solution)/shard_map/ppermute | solution.py:73
  41.9 23.9 %collective-permute-start.3 = (bf16[8,64,1024]{2,1,0:T(8,128)(2,1)S(1)}, bf16[8,64,1024]{2,1,0:T(8,128)(2,1)S(1)}, u32[]{:S(2)}, u32[]{:S(2)}) collective-permute-start(bf16[8,64,1024]{2,1,0:T(8,128)(2,1)S(1)} %pad_maximum_fusion.refs_0_), channel_id=1, source_target_pairs={{0,4},{1,5},{2,6},{3,7},{4,8},{5,9},{6,10},{7,11},{8,12},{9,13},{1... | collective-permute-start | bytes 3145736 | tf_op jit(solution)/shard_map/ppermute | solution.py:84
  46.5 20.5 %collective-permute-start.4 = (bf16[8,64,1024]{2,1,0:T(8,128)(2,1)S(1)}, bf16[8,64,1024]{2,1,0:T(8,128)(2,1)S(1)}, u32[]{:S(2)}, u32[]{:S(2)}) collective-permute-start(bf16[8,64,1024]{2,1,0:T(8,128)(2,1)S(1)} %pad_maximum_fusion.refs_0_), channel_id=1, source_target_pairs={{0,28},{1,29},{2,30},{3,31},{4,0},{5,1},{6,2},{7,3},{8,4},{9,5},{1... | collective-permute-start | bytes 3145736 | tf_op jit(solution)/shard_map/ppermute | solution.py:85
  67.0 17.8 %collective-permute-start.5 = (bf16[8,64,1024]{2,1,0:T(8,128)(2,1)S(1)}, bf16[8,64,1024]{2,1,0:T(8,128)(2,1)S(1)}, u32[]{:S(2)}, u32[]{:S(2)}) collective-permute-start(bf16[8,64,1024]{2,1,0:T(8,128)(2,1)S(1)} %collective-permute-done.3.refs_1_), channel_id=1, source_target_pairs={{0,4},{1,5},{2,6},{3,7},{4,8},{5,9},{6,10},{7,11},{8,12},{9,13},{1... | collective-permute-start | bytes 3145736 | tf_op jit(solution)/shard_map/ppermute | solution.py:84
  69.0 17.8 %collective-permute-start.6 = (bf16[8,64,1024]{2,1,0:T(8,128)(2,1)S(1)}, bf16[8,64,1024]{2,1,0:T(8,128)(2,1)S(1)}, u32[]{:S(2)}, u32[]{:S(2)}) collective-permute-start(bf16[8,64,1024]{2,1,0:T(8,128)(2,1)S(1)} %collective-permute-done.4.refs_2_), channel_id=1, source_target_pairs={{0,28},{1,29},{2,30},{3,31},{4,0},{5,1},{6,2},{7,3},{8,4},{9,5},{1... | collective-permute-start | bytes 3145736 | tf_op jit(solution)/shard_map/ppermute | solution.py:85
  84.8 17.0 %collective-permute-start.7 = (bf16[8,64,1024]{2,1,0:T(8,128)(2,1)S(1)}, bf16[8,64,1024]{2,1,0:T(8,128)(2,1)S(1)}, u32[]{:S(2)}, u32[]{:S(2)}) collective-permute-start(bf16[8,64,1024]{2,1,0:T(8,128)(2,1)S(1)} %collective-permute-done.5.refs_3_), channel_id=1, source_target_pairs={{0,4},{1,5},{2,6},{3,7},{4,8},{5,9},{6,10},{7,11},{8,12},{9,13},{1... | collective-permute-start | bytes 3145736 | tf_op jit(solution)/shard_map/ppermute | solution.py:84
  86.8 20.1 %collective-permute-start.8 = (bf16[8,64,1024]{2,1,0:T(8,128)(2,1)S(1)}, bf16[8,64,1024]{2,1,0:T(8,128)(2,1)S(1)}, u32[]{:S(2)}, u32[]{:S(2)}) collective-permute-start(bf16[8,64,1024]{2,1,0:T(8,128)(2,1)S(1)} %collective-permute-done.6.refs_4_), channel_id=1, source_target_pairs={{0,28},{1,29},{2,30},{3,31},{4,0},{5,1},{6,2},{7,3},{8,4},{9,5},{1... | collective-permute-start | bytes 3145736 | tf_op jit(solution)/shard_map/ppermute | solution.py:85
  91.3 18.1 %collective-permute-start.11 = (bf16[8,64,1024]{2,1,0:T(8,128)(2,1)S(1)}, bf16[8,64,1024]{2,1,0:T(8,128)(2,1)S(1)}, u32[]{:S(2)}, u32[]{:S(2)}) collective-permute-start(bf16[8,64,1024]{2,1,0:T(8,128)(2,1)S(1)} %pad_maximum_fusion.refs_0_), channel_id=1, source_target_pairs={{0,32},{32,0},{1,33},{33,1},{2,34},{34,2},{3,35},{35,3},{4,36},{36... | collective-permute-start | bytes 3145736 | tf_op jit(solution)/shard_map/ppermute | solution.py:89
  96.0 15.4 %collective-permute-start.12 = (bf16[8,64,1024]{2,1,0:T(8,128)(2,1)S(1)}, bf16[8,64,1024]{2,1,0:T(8,128)(2,1)S(1)}, u32[]{:S(2)}, u32[]{:S(2)}) collective-permute-start(bf16[8,64,1024]{2,1,0:T(8,128)(2,1)S(1)} %collective-permute-done.3.refs_1_), channel_id=1, source_target_pairs={{0,32},{32,0},{1,33},{33,1},{2,34},{34,2},{3,35},{35,3},{4,36},{36... | collective-permute-start | bytes 3145736 | tf_op jit(solution)/shard_map/ppermute | solution.py:89
  97.9 20.2 %collective-permute-start.13 = (bf16[8,64,1024]{2,1,0:T(8,128)(2,1)S(1)}, bf16[8,64,1024]{2,1,0:T(8,128)(2,1)S(1)}, u32[]{:S(2)}, u32[]{:S(2)}) collective-permute-start(bf16[8,64,1024]{2,1,0:T(8,128)(2,1)S(1)} %collective-permute-done.4.refs_2_), channel_id=1, source_target_pairs={{0,32},{32,0},{1,33},{33,1},{2,34},{34,2},{3,35},{35,3},{4,36},{36... | collective-permute-start | bytes 3145736 | tf_op jit(solution)/shard_map/ppermute | solution.py:89
  101.9 18.2 %collective-permute-start.14 = (bf16[8,64,1024]{2,1,0:T(8,128)(2,1)S(1)}, bf16[8,64,1024]{2,1,0:T(8,128)(2,1)S(1)}, u32[]{:S(2)}, u32[]{:S(2)}) collective-permute-start(bf16[8,64,1024]{2,1,0:T(8,128)(2,1)S(1)} %collective-permute-done.5.refs_3_), channel_id=1, source_target_pairs={{0,32},{32,0},{1,33},{33,1},{2,34},{34,2},{3,35},{35,3},{4,36},{36... | collective-permute-start | bytes 3145736 | tf_op jit(solution)/shard_map/ppermute | solution.py:89
  106.9 20.2 %collective-permute-start.15 = (bf16[8,64,1024]{2,1,0:T(8,128)(2,1)S(1)}, bf16[8,64,1024]{2,1,0:T(8,128)(2,1)S(1)}, u32[]{:S(2)}, u32[]{:S(2)}) collective-permute-start(bf16[8,64,1024]{2,1,0:T(8,128)(2,1)S(1)} %collective-permute-done.6.refs_4_), channel_id=1, source_target_pairs={{0,32},{32,0},{1,33},{33,1},{2,34},{34,2},{3,35},{35,3},{4,36},{36... | collective-permute-start | bytes 3145736 | tf_op jit(solution)/shard_map/ppermute | solution.py:89
  109.5 13.2 %collective-permute-start.9 = (bf16[4,64,1024]{2,1,0:T(8,128)(2,1)S(1)}, bf16[4,64,1024]{2,1,0:T(8,128)(2,1)S(1)}, u32[]{:S(2)}, u32[]{:S(2)}) collective-permute-start(bf16[4,64,1024]{2,1,0:T(8,128)(2,1)S(1)} %slice.16), channel_id=1, source_target_pairs={{0,4},{1,5},{2,6},{3,7},{4,8},{5,9},{6,10},{7,11},{8,12},{9,13},{1... | collective-permute-start | bytes 1572872 | tf_op jit(solution)/shard_map/ppermute | solution.py:87
  111.4 13.2 %collective-permute-start.10 = (bf16[4,64,1024]{2,1,0:T(8,128)(2,1)S(1)}, bf16[4,64,1024]{2,1,0:T(8,128)(2,1)S(1)}, u32[]{:S(2)}, u32[]{:S(2)}) collective-permute-start(bf16[4,64,1024]{2,1,0:T(8,128)(2,1)S(1)} %slice.17), channel_id=1, source_target_pairs={{0,28},{1,29},{2,30},{3,31},{4,0},{5,1},{6,2},{7,3},{8,4},{9,5},{1... | collective-permute-start | bytes 1572872 | tf_op jit(solution)/shard_map/ppermute | solution.py:88
  118.1 10.5 %collective-permute-start.16 = (bf16[8,64,1024]{2,1,0:T(8,128)(2,1)S(1)}, bf16[8,64,1024]{2,1,0:T(8,128)(2,1)S(1)}, u32[]{:S(2)}, u32[]{:S(2)}) collective-permute-start(bf16[8,64,1024]{2,1,0:T(8,128)(2,1)S(1)} %collective-permute-done.7.refs_5_), channel_id=1, source_target_pairs={{0,32},{32,0},{1,33},{33,1},{2,34},{34,2},{3,35},{35,3},{4,36},{36... | collective-permute-start | bytes 3145736 | tf_op jit(solution)/shard_map/ppermute | solution.py:89
  120.1 8.5 %collective-permute-start.17 = (bf16[8,64,1024]{2,1,0:T(8,128)(2,1)S(1)}, bf16[8,64,1024]{2,1,0:T(8,128)(2,1)S(1)}, u32[]{:S(2)}, u32[]{:S(2)}) collective-permute-start(bf16[8,64,1024]{2,1,0:T(8,128)(2,1)S(1)} %collective-permute-done.8.refs_6_), channel_id=1, source_target_pairs={{0,32},{32,0},{1,33},{33,1},{2,34},{34,2},{3,35},{35,3},{4,36},{36... | collective-permute-start | bytes 3145736 | tf_op jit(solution)/shard_map/ppermute | solution.py:89
  122.7 4.4 %collective-permute-start.18 = (bf16[4,64,1024]{2,1,0:T(8,128)(2,1)S(1)}, bf16[4,64,1024]{2,1,0:T(8,128)(2,1)S(1)}, u32[]{:S(2)}, u32[]{:S(2)}) collective-permute-start(bf16[4,64,1024]{2,1,0:T(8,128)(2,1)S(1)} %collective-permute-done.9.refs_7_), channel_id=1, source_target_pairs={{0,32},{32,0},{1,33},{33,1},{2,34},{34,2},{3,35},{35,3},{4,36},{36... | collective-permute-start | bytes 1572872 | tf_op jit(solution)/shard_map/ppermute | solution.py:89
  124.7 3.9 %collective-permute-start.19 = (bf16[4,64,1024]{2,1,0:T(8,128)(2,1)S(1)}, bf16[4,64,1024]{2,1,0:T(8,128)(2,1)S(1)}, u32[]{:S(2)}, u32[]{:S(2)}) collective-permute-start(bf16[4,64,1024]{2,1,0:T(8,128)(2,1)S(1)} %collective-permute-done.10.refs_8_), channel_id=1, source_target_pairs={{0,32},{32,0},{1,33},{33,1},{2,34},{34,2},{3,35},{35,3},{4,36},{36... | collective-permute-start | bytes 1572872 | tf_op jit(solution)/shard_map/ppermute | solution.py:89
  136.6 5.6 %collective-permute-start.20 = (bf16[32,2048]{1,0:T(8,128)(2,1)S(1)}, bf16[32,2048]{1,0:T(8,128)(2,1)S(1)}, u32[]{:S(2)}, u32[]{:S(2)}) collective-permute-start(bf16[32,2048]{1,0:T(8,128)(2,1)S(1)} %get-tuple-element.47), channel_id=1, source_target_pairs={{0,128},{1,129},{2,130},{3,131},{4,132},{5,133},{6,134},{7,135},{8... | collective-permute-start | bytes 393224 | tf_op jit(solution)/shard_map/ppermute | solution.py:309
  147.8 0.7 collective-permute-start.21
  153.9 0.8 collective-permute-start.22
  167.9 12.1 %collective-permute-start.23 = (bf16[32,2048]{1,0:T(8,128)(2,1)S(1)}, bf16[32,2048]{1,0:T(8,128)(2,1)S(1)}, u32[]{:S(2)}, u32[]{:S(2)}) collective-permute-start(bf16[32,2048]{1,0:T(8,128)(2,1)S(1)} %get-tuple-element.57), channel_id=1, source_target_pairs={{384,256},{385,257},{386,258},{387,259},{388,260},{389,261},{390,2... | collective-permute-start | bytes 393224 | tf_op jit(solution)/shard_map/ppermute | solution.py:322
  194.3 0.7 collective-permute-start.24
  202.7 18.4 %collective-permute-start.25 = (bf16[32,2048]{1,0:T(8,128)(2,1)S(1)}, bf16[32,2048]{1,0:T(8,128)(2,1)S(1)}, u32[]{:S(2)}, u32[]{:S(2)}) collective-permute-start(bf16[32,2048]{1,0:T(8,128)(2,1)S(1)} %get-tuple-element.61), channel_id=1, source_target_pairs={{128,0},{129,1},{130,2},{131,3},{132,4},{133,5},{134,6},{135,7},{1... | collective-permute-start | bytes 393224 | tf_op jit(solution)/shard_map/ppermute | solution.py:322
  256.6 64.8 %copy-start.3 = (f32[1,64,1024]{2,1,0:T(8,128)S(1)}, f32[1,64,1024]{2,1,0:T(8,128)}, u32[]{:S(2)}) copy-start(f32[1,64,1024]{2,1,0:T(8,128)} %param.15) | copy-start | bytes 786436
  256.6 64.8 %copy-start.5 = (f32[1,64,1024]{2,1,0:T(8,128)S(1)}, f32[1,64,1024]{2,1,0:T(8,128)}, u32[]{:S(2)}) copy-start(f32[1,64,1024]{2,1,0:T(8,128)} %param.16) | copy-start | bytes 786436
  256.6 64.8 %copy-start.6 = (f32[1,64,1024]{2,1,0:T(8,128)S(1)}, f32[1,64,1024]{2,1,0:T(8,128)}, u32[]{:S(2)}) copy-start(f32[1,64,1024]{2,1,0:T(8,128)} %param.17) | copy-start | bytes 786436
  321.6 6.3 %collective-permute-start.26 = (bf16[64,1024]{1,0:T(8,128)(2,1)S(1)}, bf16[64,1024]{1,0:T(8,128)(2,1)S(1)}, u32[]{:S(2)}, u32[]{:S(2)}) collective-permute-start(bf16[64,1024]{1,0:T(8,128)(2,1)S(1)} %fusion.8), channel_id=1, source_target_pairs={{32,0},{64,32},{96,64},{128,96},{160,128},{192,160},{224,192},{256... | collective-permute-start | bytes 393224 | tf_op jit(solution)/shard_map/ppermute | solution.py:353
  (4 other events, 69.7 us)
Sparse Core Ops, SparseCore 0:
  180.9 75.5 all-gather.3

commit v3 on v2

--- a/solution.py
+++ b/solution.py
@@ -16,6 +16,7 @@
 LAYERS = ZL * C
 RING = 8
 PIECES = RING + 1
+HALF = RING // 2
 OFFSETS = (0, 1, -1, 2, -2, 3, -3, 4)
 KV_HEADS = 4
 GROUPS = 4
@@ -59,7 +60,17 @@
     return everywhere(target)
 
 
-def gathered_weights(own, beside):
+def line_groups():
+    def place(zl, c, y, zh):
+        return flat(0, zl, c, y, zh)
+
+    along_y = [[place(zl, 0, y, zh) for y in range(Y)] for zl in range(ZL) for zh in range(ZH)]
+    along_z = [[place(z % 2, 1, y, z // 2) for z in range(RING)] for y in range(Y)]
+    return along_y + along_z
+
+
+def first_gather(master):
+    own = master[0].astype(BF16)
     c, y = lax.axis_index("c"), lax.axis_index("y")
     zl, zh = lax.axis_index("zl"), lax.axis_index("zh")
     rows, cols = own.shape
@@ -76,62 +87,67 @@
             piece = jnp.concatenate([low, high], axis=0)
         else:
             piece = jnp.stack([low, high], axis=1).reshape(-1, rows, cols)
-    pieces = [piece]
-    up = down = piece
+    return piece
+
+
+def line_gather(piece):
+    return lax.all_gather(
+        piece[:HALF], "r", axis=0, tiled=True, axis_index_groups=line_groups()
+    )
+
+
+def other_core(block):
+    return lax.ppermute(block, "c", [(0, 1), (1, 0)])
+
+
+def ring_gather(piece, lower, beside):
+    pieces, others = [piece[HALF:]], []
+    arrived = [pieces[0]] * 2
     for step in range(1, 4):
-        if step == 2:
-            up, down, ready = lax.optimization_barrier((up, down, beside(piece)))
-        up = lax.ppermute(up, AXES, ring_route(1))
-        down = lax.ppermute(down, AXES, ring_route(-1))
-        pieces += [up, down]
-    pieces.append(lax.ppermute(up[:4], AXES, ring_route(1)))
-    pieces.append(lax.ppermute(down[4:], AXES, ring_route(-1)))
-    others = [lax.ppermute(p, "c", [(0, 1), (1, 0)]) for p in pieces]
-    return pieces + others, ready
-
-
-def half(pieces, index, low):
-    if index == RING - 1:
-        return pieces[index + low]
-    return pieces[index].at[pl.ds(4 * low, 4)]
-
-
-def fetch_weights(pieces, w, sems, order):
-    c, y = lax.axis_index("c"), lax.axis_index("y")
-    zl = lax.axis_index("zl")
-    z = 2 * lax.axis_index("zh") + zl
-
-    def start(first, second, parity):
-        for layer in order:
-            for i, offset in enumerate(OFFSETS):
-                if layer % 2 == 0:
-                    there = lax.rem(y - offset + 2 * RING, RING)
-                    pltpu.make_async_copy(
-                        half(first, i, layer // 2),
-                        w.at[layer, there // 2, lax.rem(there, 2)],
-                        sems.at[layer],
-                    ).start()
-                elif (parity + offset) % 2 == layer // 2:
-                    there = lax.rem(z - offset + 2 * RING, RING)
-                    for low in range(2):
-                        pltpu.make_async_copy(
-                            half(second, i, low),
-                            w.at[layer, :, low, there // 2],
-                            sems.at[layer],
-                        ).start()
-
-    for core in range(C):
-        for parity in range(ZL):
-
-            @pl.when((c == core) & (zl == parity))
-            def _():
-                mine, others = pieces[:PIECES], pieces[PIECES:]
-                first, second = (mine, others) if core == 0 else (others, mine)
-                start(first, second, parity)
-
-
-def wait_weights(w, sems, layer):
-    pltpu.make_async_copy(w.at[layer], w.at[layer], sems.at[layer]).wait()
+        up = lax.ppermute(arrived[0], AXES, ring_route(1))
+        down = lax.ppermute(arrived[1], AXES, ring_route(-1))
+        news = [other_core(p) for p in pieces[len(others) :]]
+        if step == 1:
+            up, down, news, ready = lax.optimization_barrier((up, down, news, beside(piece)))
+        else:
+            up, down, news = lax.optimization_barrier((up, down, news))
+        others += news
+        arrived = [up, down]
+        pieces += arrived
+    last = lax.ppermute(up, AXES, ring_route(1))
+    lower, _ = lax.optimization_barrier((lower, down))
+    news = [other_core(p) for p in pieces[len(others) :]]
+    lower_other = other_core(lower)
+    last, news, lower_other = lax.optimization_barrier((last, news, lower_other))
+    others += [*news, other_core(last)]
+    pieces.append(last)
+    return [lower, *pieces], [lower_other, *others], ready
+
+
+def assemble_kernel(*refs):
+    pieces, (w, sem) = refs[: 2 * PIECES], refs[2 * PIECES :]
+    y = lax.axis_index("y")
+    z = 2 * lax.axis_index("zh") + lax.axis_index("zl")
+
+    def start(first, second):
+        pltpu.make_async_copy(first[0], w.at[0], sem).start()
+        for high in range(ZH):
+            for low in range(ZL):
+                source = second[0].at[high, low]
+                pltpu.make_async_copy(source, w.at[2 * low + 1, :, 0, high], sem).start()
+        for i, offset in enumerate(OFFSETS):
+            there = lax.rem(y - offset + 2 * RING, RING)
+            target = w.at[2, there // 2, lax.rem(there, 2)]
+            pltpu.make_async_copy(first[1 + i], target, sem).start()
+            there = lax.rem(z - offset + 2 * RING, RING)
+            target = w.at[2 * lax.rem(there, 2) + 1, :, 1, there // 2]
+            pltpu.make_async_copy(second[1 + i], target, sem).start()
+
+    mine, others = pieces[:PIECES], pieces[PIECES:]
+    c = lax.axis_index("c")
+    pl.when(c == 0)(functools.partial(start, mine, others))
+    pl.when(c == 1)(functools.partial(start, others, mine))
+    pltpu.make_async_copy(w, w, sem).wait()
 
 
 def head(block, index):
@@ -212,25 +228,18 @@
 
 VMEM = pl.BlockSpec(memory_space=pltpu.VMEM)
 ANY = pl.BlockSpec(memory_space=pl.ANY)
-PARAMS = dict(vmem_limit_bytes=16 * 1024 * 1024)
-
-
-def assemble_kernel(*refs):
-    pieces, (w, sems) = refs[: 2 * PIECES], refs[2 * PIECES :]
-    fetch_weights(pieces, w, sems, range(LAYERS))
-    for layer in range(LAYERS):
-        wait_weights(w, sems, layer)
+PARAMS = dict(vmem_limit_bytes=8 * 1024 * 1024)
 
 
 def assembled(pieces):
-    rows, columns = pieces[0].shape[1:]
+    rows, columns = pieces[0].shape[-2:]
     return pl.pallas_call(
         assemble_kernel,
         out_shape=pltpu.VMEM((LAYERS, Y // 2, 2, ZH, rows, columns), BF16),
         in_specs=[ANY] * (2 * PIECES),
         out_specs=VMEM,
-        scratch_shapes=[pltpu.SemaphoreType.DMA((LAYERS,))],
-        compiler_params=pltpu.CompilerParams(**PARAMS),
+        scratch_shapes=[pltpu.SemaphoreType.DMA],
+        compiler_params=pltpu.CompilerParams(vmem_limit_bytes=2 * 1024 * 1024),
         name="assemble",
     )(*pieces)
 
@@ -281,7 +290,7 @@
     return value
 
 
-def body(inputs, upstream, segments, gains, master, moment, second):
+def body(piece, lower, inputs, upstream, segments, gains, master, moment, second):
     stage = lax.axis_index("x")
     which = lax.axis_index("zl") * C + lax.axis_index("c")
     length, width = inputs.shape[1:]
@@ -299,8 +308,10 @@
         is_stage = tuple(stage == i for i in range(X))
         return plane_gains, mask, first, last, is_stage
 
-    pieces, (plane_gains, mask, first, last, is_stage) = gathered_weights(master[0].astype(BF16), beside)
-    w = assembled(pieces)
+    lower = lower.reshape(Y // 2, 2, HALF, rows, columns)
+    mine, others, ready = ring_gather(piece, lower, beside)
+    plane_gains, mask, first, last, is_stage = ready
+    w = assembled([*mine, *others])
 
     held = first
     for turn in range(X):
@@ -356,11 +367,21 @@
 
 def solution(mesh):
     fine = Mesh(mesh.devices.reshape(X, ZL, C, Y, ZH), AXES)
+    lines = Mesh(mesh.devices.reshape(X, ZL * C * Y * ZH), ("x", "r"))
     state = P(SECTION, DP, None)
-    return jax.shard_map(
+    each, each_line = P(AXES), P(("x", "r"))
+    first = jax.shard_map(
+        first_gather, mesh=fine, in_specs=(state,), out_specs=each, check_vma=False
+    )
+    second = jax.shard_map(
+        line_gather, mesh=lines, in_specs=(each_line,), out_specs=each_line, check_vma=False
+    )
+    rest = jax.shard_map(
         body,
         mesh=fine,
         in_specs=(
+            each,
+            each,
             P(None, DP, None),
             P(None, DP, None),
             P(None, DP),
@@ -372,3 +393,19 @@
         out_specs=(state,) * 4,
         check_vma=False,
     )
+
+    def program(inputs, upstream, segments, gains, master, moment, second_moment):
+        piece = first(master)
+        return rest(
+            piece,
+            second(piece),
+            inputs,
+            upstream,
+            segments,
+            gains,
+            master,
+            moment,
+            second_moment,
+        )
+
+    return program

time: 336 us -> 339 us (level)
  local copies, waits for them, and re-layouts: 11.7 us -> 23.4 us
  starting transfers between devices: 86.2 us -> 79.3 us
    unnamed x17 -> x45, local copies, waits for them, and re-layouts: 7.25 us -> 20.5 us
    ppermute x20 -> x19, starting transfers between devices: 76.4 us -> 69.5 us  [the longest x9 22 us: other_core(): return lax.ppermute(block, 'c', [(0, 1), (1, 0)])]
    ppermute x20 -> x19, waiting for transfers between devices: 33.2 us -> 33.1 us  [the longest x3 16.6 us: first_gather(): other = lax.ppermute(piece, AXES, swap_route(bit))]
where the time goes in v3:
time: 339 us; the launch traced here: 338 us
  blocking collectives  94.8 us (28%)
  starting transfers between devices  79.3 us (23%)
  waiting for transfers between devices  59.8 us (18%)
  Pallas kernels  55.4 us (16%)
  local copies, waits for them, and re-layouts  23.4 us (7%)
  between operations  15.4 us (5%)
  other arithmetic  6.28 us (2%)
  matrix products  3.58 us (1%)
    all_to_all x5, blocking collectives, exchange(): return lax.all_to_all(block, axes, split_axis=0, concat_axis=0, tiled=True)  89.8 us
    pallas_call x4, Pallas kernels, run_backward(): pl.pallas_call(backward_kernel, out_shape=(jax.ShapeDtypeStruct((length,...  30.9 us
    pallas_call x4, Pallas kernels, run_forward(): pl.pallas_call(forward_kernel, out_shape=(jax.ShapeDtypeStruct((length, w...  23.1 us
    ppermute x9, starting transfers between devices, other_core(): return lax.ppermute(block, 'c', [(0, 1), (1, 0)])  22 us
    ppermute x3, starting transfers between devices, ring_gather(): down = lax.ppermute(arrived[1], AXES, ring_route(-1))  20.7 us
    unnamed x45, local copies, waits for them, and re-layouts  20.5 us
    ppermute x3, waiting for transfers between devices, body(): arrived = lax.ppermute(dx, 'x', [(here, here - 1)])  17.3 us
    ppermute x3, waiting for transfers between devices, first_gather(): other = lax.ppermute(piece, AXES, swap_route(bit))  16.6 us
  transfers between devices with their start and end apart: 28, of which 13 were waited for; matrix products, arithmetic and copies ran while one was open for 1% of the time, Pallas kernels for 7%

profile of v3, /device:TPU:1, one launch (start us, length us, event | category | flops | bytes accessed | tf_op | source)
XLA Modules:
  0.0 337.9 jit_solution(9858880416262858910)
XLA Ops:
  8.2 8.3 %collective-permute-start = (bf16[1,64,1024]{2,1,0:T(8,128)(2,1)S(1)}, bf16[1,64,1024]{2,1,0:T(8,128)(2,1)S(1)}, u32[]{:S(2)}, u32[]{:S(2)}) collective-permute-start(bf16[1,64,1024]{2,1,0:T(8,128)(2,1)S(1)} %convert_element_type.27), channel_id=1, source_target_pairs={{0,2},{1,3},{2,0},{3,1},{4,6},{5,7},{6,4},{7,5},{8,10},{9,11},{10,... | collective-permute-start | bytes 393224 | tf_op jit(solution)/shard_map/ppermute | solution.py:84
  20.0 5.4 %collective-permute-start.1 = (bf16[2,64,1024]{2,1,0:T(8,128)(2,1)S(1)}, bf16[2,64,1024]{2,1,0:T(8,128)(2,1)S(1)}, u32[]{:S(2)}, u32[]{:S(2)}) collective-permute-start(bf16[2,64,1024]{2,1,0:T(8,128)(2,1)S(1)} %pad_maximum_fusion.1), channel_id=1, source_target_pairs={{0,1},{1,0},{2,3},{3,2},{4,5},{5,4},{6,7},{7,6},{8,9},{9,8},{10,11... | collective-permute-start | bytes 786440 | tf_op jit(solution)/shard_map/ppermute | solution.py:84
  25.4 6.2 %collective-permute-done.1 = bf16[2,64,1024]{2,1,0:T(8,128)(2,1)S(1)} collective-permute-done((bf16[2,64,1024]{2,1,0:T(8,128)(2,1)S(1)}, bf16[2,64,1024]{2,1,0:T(8,128)(2,1)S(1)}, u32[]{:S(2)}, u32[]{:S(2)}) %collective-permute-start.1) | collective-permute-done | bytes 262176 | tf_op jit(solution)/shard_map/ppermute | solution.py:84
  33.7 8.0 %collective-permute-done.2 = bf16[4,64,1024]{2,1,0:T(8,128)(2,1)S(1)} collective-permute-done((bf16[4,64,1024]{2,1,0:T(8,128)(2,1)S(1)}, bf16[4,64,1024]{2,1,0:T(8,128)(2,1)S(1)}, u32[]{:S(2)}, u32[]{:S(2)}) %collective-permute-start.2) | collective-permute-done | bytes 524320 | tf_op jit(solution)/shard_map/ppermute | solution.py:84
  42.7 4.6 %collective-permute-start.3 = (bf16[4,64,1024]{2,1,0:T(8,128)(2,1)S(1)}, bf16[4,64,1024]{2,1,0:T(8,128)(2,1)S(1)}, u32[]{:S(2)}, u32[]{:S(2)}) collective-permute-start(bf16[4,64,1024]{2,1,0:T(8,128)(2,1)S(1)} %get-tuple-element.97.refs_1_), channel_id=1, source_target_pairs={{0,4},{1,5},{2,6},{3,7},{4,8},{5,9},{6,10},{7,11},{8,12},{9,13},{1... | collective-permute-start | bytes 1572872 | tf_op jit(solution)/shard_map/ppermute | solution.py:107
  47.3 8.8 %collective-permute-start.4 = (bf16[4,64,1024]{2,1,0:T(8,128)(2,1)S(1)}, bf16[4,64,1024]{2,1,0:T(8,128)(2,1)S(1)}, u32[]{:S(2)}, u32[]{:S(2)}) collective-permute-start(bf16[4,64,1024]{2,1,0:T(8,128)(2,1)S(1)} %get-tuple-element.97.refs_1_), channel_id=1, source_target_pairs={{0,28},{1,29},{2,30},{3,31},{4,0},{5,1},{6,2},{7,3},{8,4},{9,5},{1... | collective-permute-start | bytes 1572872 | tf_op jit(solution)/shard_map/ppermute | solution.py:108
  59.2 5.0 %all-gather.1.gain_ref = f32[4,1,2048]{2,1,0:T(1,128)S(1)} all-gather(f32[1,1,2048]{2,1,0:T(1,128)S(1)} %bitcast.75), channel_id=2, replica_groups=mesh['x'=4,'zl'=2,'c'=2,'y'=8,'zh'=4] {'zl','c'}, dimensions={0}, use_global_device_ids=true | all-gather | bytes 40960 | tf_op jit(solution)/shard_map/all_gather | solution.py:301
  67.3 6.5 %collective-permute-start.7 = (bf16[4,64,1024]{2,1,0:T(8,128)(2,1)S(1)}, bf16[4,64,1024]{2,1,0:T(8,128)(2,1)S(1)}, u32[]{:S(2)}, u32[]{:S(2)}) collective-permute-start(bf16[4,64,1024]{2,1,0:T(8,128)(2,1)S(1)} %collective-permute-done.4.refs_3_), channel_id=1, source_target_pairs={{0,28},{1,29},{2,30},{3,31},{4,0},{5,1},{6,2},{7,3},{8,4},{9,5},{1... | collective-permute-start | bytes 1572872 | tf_op jit(solution)/shard_map/ppermute | solution.py:108
  78.2 5.8 %collective-permute-done.6.refs_4_ = bf16[4,64,1024]{2,1,0:T(8,128)(2,1)S(1)} collective-permute-done((bf16[4,64,1024]{2,1,0:T(8,128)(2,1)S(1)}, bf16[4,64,1024]{2,1,0:T(8,128)(2,1)S(1)}, u32[]{:S(2)}, u32[]{:S(2)}) %collective-permute-start.6) | collective-permute-done | bytes 524320 | tf_op jit(solution)/shard_map/ppermute | solution.py:107
  88.2 5.4 %collective-permute-start.11 = (bf16[4,64,1024]{2,1,0:T(8,128)(2,1)S(1)}, bf16[4,64,1024]{2,1,0:T(8,128)(2,1)S(1)}, u32[]{:S(2)}, u32[]{:S(2)}) collective-permute-start(bf16[4,64,1024]{2,1,0:T(8,128)(2,1)S(1)} %collective-permute-done.7.refs_5_), channel_id=1, source_target_pairs={{0,28},{1,29},{2,30},{3,31},{4,0},{5,1},{6,2},{7,3},{8,4},{9,5},{1... | collective-permute-start | bytes 1572872 | tf_op jit(solution)/shard_map/ppermute | solution.py:108
  98.8 2.8 collective-permute-done.10.refs_6_
  104.9 3.8 %collective-permute-start.17 = (bf16[4,2,4,64,1024]{4,3,2,1,0:T(8,128)(2,1)}, bf16[4,2,4,64,1024]{4,3,2,1,0:T(8,128)(2,1)S(1)}, u32[]{:S(2)}, u32[]{:S(2)}) collective-permute-start(bf16[4,2,4,64,1024]{4,3,2,1,0:T(8,128)(2,1)} %bitcast.64), channel_id=1, source_target_pairs={{0,32},{32,0},{1,33},{33,1},{2,34},{34,2},{3,35},{35,3},{4,36},{36... | collective-permute-start | bytes 12582920 | tf_op jit(solution)/shard_map/ppermute | solution.py:100
  115.9 4.8 %collective-permute-done.14.refs_8_ = bf16[4,64,1024]{2,1,0:T(8,128)(2,1)S(1)} collective-permute-done((bf16[4,64,1024]{2,1,0:T(8,128)(2,1)S(1)}, bf16[4,64,1024]{2,1,0:T(8,128)(2,1)S(1)}, u32[]{:S(2)}, u32[]{:S(2)}) %collective-permute-start.14) | collective-permute-done | bytes 524320 | tf_op jit(solution)/shard_map/ppermute | solution.py:117
  134.3 6.6 %stage_forward.4 = (bf16[32,2048]{1,0:T(8,128)(2,1)S(1)}, bf16[4,32,2048]{2,1,0:T(8,128)(2,1)}, bf16[4,32,2048]{2,1,0:T(8,128)(2,1)}, bf16[4,32,1024]{2,1,0:T(8,128)(2,1)}, f32[4,32,512]{2,1,0:T(8,128)}) custom-call(bf16[32,2048]{1,0:T(8,128)(2,1)S(1)} %get-tuple-element.58.x_ref, f32[4,1,2048]{2,1,0:T(1,128)S(1)} %all-gather.1.gain_ref, ...), custom_call_target="tpu_custom_call" | custom-call | tf_op jit(solution)/shard_map/stage_forward/pallas_call | solution.py:250
  140.9 3.1 collective-permute-start.19
  146.6 5.6 %stage_forward.5 = (bf16[32,2048]{1,0:T(8,128)(2,1)S(1)}, bf16[4,32,2048]{2,1,0:T(8,128)(2,1)}, bf16[4,32,2048]{2,1,0:T(8,128)(2,1)}, bf16[4,32,1024]{2,1,0:T(8,128)(2,1)}, f32[4,32,512]{2,1,0:T(8,128)}) custom-call(bf16[32,2048]{1,0:T(8,128)(2,1)S(1)} %broadcast_select_fusion.5.x_ref, f32[4,1,2048]{2,1,0:T(1,128)S(1)} %all-gather.1.gain_ref, ...), custom_call_target="tpu_custom_call" | custom-call | tf_op jit(solution)/shard_map/stage_forward/pallas_call | solution.py:250
  152.9 5.4 %stage_forward.6 = (bf16[32,2048]{1,0:T(8,128)(2,1)S(1)}, bf16[4,32,2048]{2,1,0:T(8,128)(2,1)}, bf16[4,32,2048]{2,1,0:T(8,128)(2,1)S(1)}, bf16[4,32,1024]{2,1,0:T(8,128)(2,1)}, f32[4,32,512]{2,1,0:T(8,128)}) custom-call(bf16[32,2048]{1,0:T(8,128)(2,1)S(1)} %broadcast_select_fusion.7.x_ref, f32[4,1,2048]{2,1,0:T(1,128)S(1)} %all-gather.1.gain_ref, ...), custom_call_target="tpu_custom_call" | custom-call | tf_op jit(solution)/shard_map/stage_forward/pallas_call | solution.py:250
  159.0 5.5 %stage_forward.7 = (bf16[32,2048]{1,0:T(8,128)(2,1)}, bf16[4,32,2048]{2,1,0:T(8,128)(2,1)S(1)}, bf16[4,32,2048]{2,1,0:T(8,128)(2,1)S(1)}, bf16[4,32,1024]{2,1,0:T(8,128)(2,1)S(1)}, f32[4,32,512]{2,1,0:T(8,128)S(1)}) custom-call(bf16[32,2048]{1,0:T(8,128)(2,1)S(1)} %broadcast_select_fusion.3.x_ref, f32[4,1,2048]{2,1,0:T(1,128)S(1)} %all-gather.1.gain_ref, ...), custom_call_target="tpu_custom_call" | custom-call | tf_op jit(solution)/shard_map/stage_forward/pallas_call | solution.py:250
  164.5 7.7 %stage_backward.4 = (bf16[32,2048]{1,0:T(8,128)(2,1)S(1)}, bf16[4,32,1024]{2,1,0:T(8,128)(2,1)}) custom-call(bf16[32,2048]{1,0:T(8,128)(2,1)S(1)} %get-tuple-element.83.dy_ref, f32[4,1,2048]{2,1,0:T(1,128)S(1)} %all-gather.1.gain_ref, bf16[4,32,2048]{2,1,0:T(8,128)(2,1)S(1)} %get-tuple-element.84.xs_ref, bf16[4,32,2048]{2,1,0:T(8,128)(2,1)S(1)} %get-tuple-element.88.h_ref, ...), custom_call_target="tpu_custom_call" | custom-call | tf_op jit(solution)/shard_map/stage_backward/pallas_call | solution.py:269
  172.9 11.3 %conditional.2 = (bf16[4,32,2048]{2,1,0:T(8,128)(2,1)S(1)}) conditional(s32[]{:T(128)} %convert_element_type.29, bf16[4,32,2048]{2,1,0:T(8,128)(2,1)S(1)} %get-tuple-element.81, () %tuple.37), branch_computations={%region_0.3_spmd, %region_1.4_spmd} | conditional | bytes 1048584 | solution.py:324
  172.9 11.3 %all_to_all.36 = bf16[4,32,2048]{2,1,0:T(8,128)(2,1)S(1)} all-to-all(bf16[4,32,2048]{2,1,0:T(8,128)(2,1)S(1)} %param.2), channel_id=1, replica_groups=mesh['x'=4,'zl'=2,'c'=2,'y'=8,'zh'=4] {'zl','c'}, dimensions={0} | all-to-all | bytes 1048576 | tf_op jit(solution)/shard_map/cond/branch_0_fun/all_to_all | solution.py:283
  185.1 5.8 %copy-done.2 = bf16[4,4,2,4,64,1024]{5,4,3,2,1,0:T(8,128)(2,1)S(1)} copy-done((bf16[4,4,2,4,64,1024]{5,4,3,2,1,0:T(8,128)(2,1)S(1)}, bf16[4,4,2,4,64,1024]{5,4,3,2,1,0:T(8,128)(2,1)}, u32[]{:S(2)}) %copy-start.2) | copy-done | bytes 16777240
  190.8 7.7 %stage_backward.5 = (bf16[32,2048]{1,0:T(8,128)(2,1)S(1)}, bf16[4,32,1024]{2,1,0:T(8,128)(2,1)}) custom-call(bf16[32,2048]{1,0:T(8,128)(2,1)S(1)} %broadcast_select_fusion.6.dy_ref, f32[4,1,2048]{2,1,0:T(1,128)S(1)} %all-gather.1.gain_ref, bf16[4,32,2048]{2,1,0:T(8,128)(2,1)S(1)} %get-tuple-element.84.xs_ref, ...), custom_call_target="tpu_custom_call" | custom-call | tf_op jit(solution)/shard_map/stage_backward/pallas_call | solution.py:269
  199.4 7.7 %stage_backward.6 = (bf16[32,2048]{1,0:T(8,128)(2,1)S(1)}, bf16[4,32,1024]{2,1,0:T(8,128)(2,1)}) custom-call(bf16[32,2048]{1,0:T(8,128)(2,1)S(1)} %broadcast_select_fusion.4.dy_ref, f32[4,1,2048]{2,1,0:T(1,128)S(1)} %all-gather.1.gain_ref, bf16[4,32,2048]{2,1,0:T(8,128)(2,1)S(1)} %get-tuple-element.84.xs_ref, ...), custom_call_target="tpu_custom_call" | custom-call | tf_op jit(solution)/shard_map/stage_backward/pallas_call | solution.py:269
  208.4 17.3 %collective-permute-done.24 = bf16[32,2048]{1,0:T(8,128)(2,1)S(1)} collective-permute-done((bf16[32,2048]{1,0:T(8,128)(2,1)S(1)}, bf16[32,2048]{1,0:T(8,128)(2,1)S(1)}, u32[]{:S(2)}, u32[]{:S(2)}) %collective-permute-start.24) | collective-permute-done | bytes 131104 | tf_op jit(solution)/shard_map/ppermute | solution.py:333
  225.7 7.8 %stage_backward.7 = (bf16[32,2048]{1,0:T(8,128)(2,1)}, bf16[4,32,1024]{2,1,0:T(8,128)(2,1)S(1)}) custom-call(bf16[32,2048]{1,0:T(8,128)(2,1)S(1)} %broadcast_select_fusion.2.dy_ref, f32[4,1,2048]{2,1,0:T(1,128)S(1)} %all-gather.1.gain_ref, bf16[4,32,2048]{2,1,0:T(8,128)(2,1)S(1)} %get-tuple-element.84.xs_ref, ...), custom_call_target="tpu_custom_call" | custom-call | tf_op jit(solution)/shard_map/stage_backward/pallas_call | solution.py:269
  233.6 21.5 %all_to_all.38 = bf16[32,32,128]{2,1,0:T(8,128)(2,1)S(1)} all-to-all(bf16[32,32,128]{2,1,0:T(8,128)(2,1)S(1)} %bitcast.68), channel_id=1, replica_groups=mesh['x'=4,'zl'=2,'c'=2,'y'=8,'zh'=4] {'zl','c','y'}, dimensions={0} | all-to-all | bytes 524288 | tf_op jit(solution)/shard_map/all_to_all | solution.py:283
  255.1 4.0 %all-gather.7.cloned.1.call-done = bf16[1024,2048]{1,0:T(8,128)(2,1)} async-done(((bf16[128,2048]{1,0:T(8,128)(2,1)}), bf16[1024,2048]{1,0:T(8,128)(2,1)}) %all-gather.7.cloned.1.call-update) | async-done | bytes 4194320 | tf_op jit(solution)/shard_map/all_gather | solution.py:340
  259.1 3.6 %convolution_convert_fusion = bf16[2048,128]{1,0:T(8,128)(2,1)S(1)} fusion(bf16[1024,2048]{1,0:T(8,128)(2,1)} %all-gather.7.cloned.1.call-done, bf16[1024,128]{1,0:T(8,128)(2,1)S(1)} %bitcast.71), kind=kOutput, calls=%fused_computation | convolution fusion | flops 537133056 | bytes 4980736 | tf_op jit(solution)/shard_map/dot_general | solution.py:348
  262.7 27.2 %all_to_all.39 = bf16[32,64,128]{2,1,0:T(8,128)(2,1)S(1)} all-to-all(bf16[32,64,128]{2,1,0:T(8,128)(2,1)S(1)} %bitcast.70), channel_id=1, replica_groups=mesh['x'=4,'zl'=2,'c'=2,'y'=8,'zh'=4] {'y','zh'}, dimensions={0} | all-to-all | bytes 1048576 | tf_op jit(solution)/shard_map/all_to_all | solution.py:283
  291.3 17.4 %all_to_all.40 = f32[32,1,128]{2,1,0:T(1,128)S(1)} all-to-all(f32[32,1,128]{2,1,0:T(1,128)S(1)} %broadcast_in_dim.7), channel_id=1, replica_groups=mesh['x'=4,'zl'=2,'c'=2,'y'=8,'zh'=4] {'y','zh'}, dimensions={0} | all-to-all | bytes 32768 | tf_op jit(solution)/shard_map/all_to_all | solution.py:283
  310.0 12.3 %all_to_all.41 = f32[16,1,128]{2,1,0:T(1,128)S(1)} all-to-all(f32[16,1,128]{2,1,0:T(1,128)S(1)} %broadcast_in_dim.8), channel_id=1, replica_groups=mesh['x'=4,'zl'=2,'c'=2,'y'=8,'zh'=4] {'x','zl','c'}, dimensions={0} | all-to-all | bytes 16384 | tf_op jit(solution)/shard_map/all_to_all | solution.py:283
  (120 shorter events, 69.6 us)
Async XLA Ops:
  7.2 52.0 %copy-start.21 = (f32[1,2048]{1,0:T(1,128)S(1)}, f32[1,2048]{1,0:T(1,128)}, u32[]{:S(2)}) copy-start(f32[1,2048]{1,0:T(1,128)} %param.19) | copy-start | bytes 24580
  7.2 97.7 %all-gather.5.cloned.1.call-start = ((), (), s32[]{:S(2)}) async-start(), calls=%async_computation.6 | async-start | bytes 4718592 | tf_op jit(solution)/shard_map/all_gather | solution.py:94
  8.2 10.7 %collective-permute-start = (bf16[1,64,1024]{2,1,0:T(8,128)(2,1)S(1)}, bf16[1,64,1024]{2,1,0:T(8,128)(2,1)S(1)}, u32[]{:S(2)}, u32[]{:S(2)}) collective-permute-start(bf16[1,64,1024]{2,1,0:T(8,128)(2,1)S(1)} %convert_element_type.27), channel_id=1, source_target_pairs={{0,2},{1,3},{2,0},{3,1},{4,6},{5,7},{6,4},{7,5},{8,10},{9,11},{10,... | collective-permute-start | bytes 393224 | tf_op jit(solution)/shard_map/ppermute | solution.py:84
  20.0 11.7 %collective-permute-start.1 = (bf16[2,64,1024]{2,1,0:T(8,128)(2,1)S(1)}, bf16[2,64,1024]{2,1,0:T(8,128)(2,1)S(1)}, u32[]{:S(2)}, u32[]{:S(2)}) collective-permute-start(bf16[2,64,1024]{2,1,0:T(8,128)(2,1)S(1)} %pad_maximum_fusion.1), channel_id=1, source_target_pairs={{0,1},{1,0},{2,3},{3,2},{4,5},{5,4},{6,7},{7,6},{8,9},{9,8},{10,11... | collective-permute-start | bytes 786440 | tf_op jit(solution)/shard_map/ppermute | solution.py:84
  31.8 9.9 %collective-permute-start.2 = (bf16[4,64,1024]{2,1,0:T(8,128)(2,1)S(1)}, bf16[4,64,1024]{2,1,0:T(8,128)(2,1)S(1)}, u32[]{:S(2)}, u32[]{:S(2)}) collective-permute-start(bf16[4,64,1024]{2,1,0:T(8,128)(2,1)S(1)} %bitcast.66), channel_id=1, source_target_pairs={{0,64},{1,65},{2,66},{3,67},{4,68},{5,69},{6,70},{7,71},{8,72},{9,... | collective-permute-start | bytes 1572872 | tf_op jit(solution)/shard_map/ppermute | solution.py:84
  42.6 216.5 %all-gather.7.cloned.1.call-start = ((), (), s32[]{:S(2)}) async-start(), calls=%async_computation.7 | async-start | bytes 4718592 | tf_op jit(solution)/shard_map/all_gather | solution.py:340
  42.7 22.6 %collective-permute-start.3 = (bf16[4,64,1024]{2,1,0:T(8,128)(2,1)S(1)}, bf16[4,64,1024]{2,1,0:T(8,128)(2,1)S(1)}, u32[]{:S(2)}, u32[]{:S(2)}) collective-permute-start(bf16[4,64,1024]{2,1,0:T(8,128)(2,1)S(1)} %get-tuple-element.97.refs_1_), channel_id=1, source_target_pairs={{0,4},{1,5},{2,6},{3,7},{4,8},{5,9},{6,10},{7,11},{8,12},{9,13},{1... | collective-permute-start | bytes 1572872 | tf_op jit(solution)/shard_map/ppermute | solution.py:107
  47.3 18.0 %collective-permute-start.4 = (bf16[4,64,1024]{2,1,0:T(8,128)(2,1)S(1)}, bf16[4,64,1024]{2,1,0:T(8,128)(2,1)S(1)}, u32[]{:S(2)}, u32[]{:S(2)}) collective-permute-start(bf16[4,64,1024]{2,1,0:T(8,128)(2,1)S(1)} %get-tuple-element.97.refs_1_), channel_id=1, source_target_pairs={{0,28},{1,29},{2,30},{3,31},{4,0},{5,1},{6,2},{7,3},{8,4},{9,5},{1... | collective-permute-start | bytes 1572872 | tf_op jit(solution)/shard_map/ppermute | solution.py:108
  56.1 9.2 %collective-permute-start.5 = (bf16[4,64,1024]{2,1,0:T(8,128)(2,1)S(1)}, bf16[4,64,1024]{2,1,0:T(8,128)(2,1)S(1)}, u32[]{:S(2)}, u32[]{:S(2)}) collective-permute-start(bf16[4,64,1024]{2,1,0:T(8,128)(2,1)S(1)} %get-tuple-element.97.refs_1_), channel_id=1, source_target_pairs={{0,32},{32,0},{1,33},{33,1},{2,34},{34,2},{3,35},{35,3},{4,36},{36... | collective-permute-start | bytes 1572872 | tf_op jit(solution)/shard_map/ppermute | solution.py:100
  65.3 18.7 %collective-permute-start.6 = (bf16[4,64,1024]{2,1,0:T(8,128)(2,1)S(1)}, bf16[4,64,1024]{2,1,0:T(8,128)(2,1)S(1)}, u32[]{:S(2)}, u32[]{:S(2)}) collective-permute-start(bf16[4,64,1024]{2,1,0:T(8,128)(2,1)S(1)} %collective-permute-done.3.refs_2_), channel_id=1, source_target_pairs={{0,4},{1,5},{2,6},{3,7},{4,8},{5,9},{6,10},{7,11},{8,12},{9,13},{1... | collective-permute-start | bytes 1572872 | tf_op jit(solution)/shard_map/ppermute | solution.py:107
  67.3 17.3 %collective-permute-start.7 = (bf16[4,64,1024]{2,1,0:T(8,128)(2,1)S(1)}, bf16[4,64,1024]{2,1,0:T(8,128)(2,1)S(1)}, u32[]{:S(2)}, u32[]{:S(2)}) collective-permute-start(bf16[4,64,1024]{2,1,0:T(8,128)(2,1)S(1)} %collective-permute-done.4.refs_3_), channel_id=1, source_target_pairs={{0,28},{1,29},{2,30},{3,31},{4,0},{5,1},{6,2},{7,3},{8,4},{9,5},{1... | collective-permute-start | bytes 1572872 | tf_op jit(solution)/shard_map/ppermute | solution.py:108
  73.8 10.8 %collective-permute-start.8 = (bf16[4,64,1024]{2,1,0:T(8,128)(2,1)S(1)}, bf16[4,64,1024]{2,1,0:T(8,128)(2,1)S(1)}, u32[]{:S(2)}, u32[]{:S(2)}) collective-permute-start(bf16[4,64,1024]{2,1,0:T(8,128)(2,1)S(1)} %collective-permute-done.3.refs_2_), channel_id=1, source_target_pairs={{0,32},{32,0},{1,33},{33,1},{2,34},{34,2},{3,35},{35,3},{4,36},{36... | collective-permute-start | bytes 1572872 | tf_op jit(solution)/shard_map/ppermute | solution.py:100
  75.8 9.7 %collective-permute-start.9 = (bf16[4,64,1024]{2,1,0:T(8,128)(2,1)S(1)}, bf16[4,64,1024]{2,1,0:T(8,128)(2,1)S(1)}, u32[]{:S(2)}, u32[]{:S(2)}) collective-permute-start(bf16[4,64,1024]{2,1,0:T(8,128)(2,1)S(1)} %collective-permute-done.4.refs_3_), channel_id=1, source_target_pairs={{0,32},{32,0},{1,33},{33,1},{2,34},{34,2},{3,35},{35,3},{4,36},{36... | collective-permute-start | bytes 1572872 | tf_op jit(solution)/shard_map/ppermute | solution.py:100
  86.3 15.4 %collective-permute-start.10 = (bf16[4,64,1024]{2,1,0:T(8,128)(2,1)S(1)}, bf16[4,64,1024]{2,1,0:T(8,128)(2,1)S(1)}, u32[]{:S(2)}, u32[]{:S(2)}) collective-permute-start(bf16[4,64,1024]{2,1,0:T(8,128)(2,1)S(1)} %collective-permute-done.6.refs_4_), channel_id=1, source_target_pairs={{0,4},{1,5},{2,6},{3,7},{4,8},{5,9},{6,10},{7,11},{8,12},{9,13},{1... | collective-permute-start | bytes 1572872 | tf_op jit(solution)/shard_map/ppermute | solution.py:107
  88.2 14.3 %collective-permute-start.11 = (bf16[4,64,1024]{2,1,0:T(8,128)(2,1)S(1)}, bf16[4,64,1024]{2,1,0:T(8,128)(2,1)S(1)}, u32[]{:S(2)}, u32[]{:S(2)}) collective-permute-start(bf16[4,64,1024]{2,1,0:T(8,128)(2,1)S(1)} %collective-permute-done.7.refs_5_), channel_id=1, source_target_pairs={{0,28},{1,29},{2,30},{3,31},{4,0},{5,1},{6,2},{7,3},{8,4},{9,5},{1... | collective-permute-start | bytes 1572872 | tf_op jit(solution)/shard_map/ppermute | solution.py:108
  93.6 8.9 %collective-permute-start.12 = (bf16[4,64,1024]{2,1,0:T(8,128)(2,1)S(1)}, bf16[4,64,1024]{2,1,0:T(8,128)(2,1)S(1)}, u32[]{:S(2)}, u32[]{:S(2)}) collective-permute-start(bf16[4,64,1024]{2,1,0:T(8,128)(2,1)S(1)} %collective-permute-done.6.refs_4_), channel_id=1, source_target_pairs={{0,32},{32,0},{1,33},{33,1},{2,34},{34,2},{3,35},{35,3},{4,36},{36... | collective-permute-start | bytes 1572872 | tf_op jit(solution)/shard_map/ppermute | solution.py:100
  95.5 8.6 %collective-permute-start.13 = (bf16[4,64,1024]{2,1,0:T(8,128)(2,1)S(1)}, bf16[4,64,1024]{2,1,0:T(8,128)(2,1)S(1)}, u32[]{:S(2)}, u32[]{:S(2)}) collective-permute-start(bf16[4,64,1024]{2,1,0:T(8,128)(2,1)S(1)} %collective-permute-done.7.refs_5_), channel_id=1, source_target_pairs={{0,32},{32,0},{1,33},{33,1},{2,34},{34,2},{3,35},{35,3},{4,36},{36... | collective-permute-start | bytes 1572872 | tf_op jit(solution)/shard_map/ppermute | solution.py:100
  104.9 15.8 %collective-permute-start.17 = (bf16[4,2,4,64,1024]{4,3,2,1,0:T(8,128)(2,1)}, bf16[4,2,4,64,1024]{4,3,2,1,0:T(8,128)(2,1)S(1)}, u32[]{:S(2)}, u32[]{:S(2)}) collective-permute-start(bf16[4,2,4,64,1024]{4,3,2,1,0:T(8,128)(2,1)} %bitcast.64), channel_id=1, source_target_pairs={{0,32},{32,0},{1,33},{33,1},{2,34},{34,2},{3,35},{35,3},{4,36},{36... | collective-permute-start | bytes 12582920 | tf_op jit(solution)/shard_map/ppermute | solution.py:100
  108.7 12.0 %collective-permute-start.14 = (bf16[4,64,1024]{2,1,0:T(8,128)(2,1)S(1)}, bf16[4,64,1024]{2,1,0:T(8,128)(2,1)S(1)}, u32[]{:S(2)}, u32[]{:S(2)}) collective-permute-start(bf16[4,64,1024]{2,1,0:T(8,128)(2,1)S(1)} %collective-permute-done.10.refs_6_), channel_id=1, source_target_pairs={{0,4},{1,5},{2,6},{3,7},{4,8},{5,9},{6,10},{7,11},{8,12},{9,13},{1... | collective-permute-start | bytes 1572872 | tf_op jit(solution)/shard_map/ppermute | solution.py:117
  111.3 9.4 %collective-permute-start.15 = (bf16[4,64,1024]{2,1,0:T(8,128)(2,1)S(1)}, bf16[4,64,1024]{2,1,0:T(8,128)(2,1)S(1)}, u32[]{:S(2)}, u32[]{:S(2)}) collective-permute-start(bf16[4,64,1024]{2,1,0:T(8,128)(2,1)S(1)} %collective-permute-done.10.refs_6_), channel_id=1, source_target_pairs={{0,32},{32,0},{1,33},{33,1},{2,34},{34,2},{3,35},{35,3},{4,36},{36... | collective-permute-start | bytes 1572872 | tf_op jit(solution)/shard_map/ppermute | solution.py:100
  114.0 6.7 %collective-permute-start.16 = (bf16[4,64,1024]{2,1,0:T(8,128)(2,1)}, bf16[4,64,1024]{2,1,0:T(8,128)(2,1)S(1)}, u32[]{:S(2)}, u32[]{:S(2)}) collective-permute-start(bf16[4,64,1024]{2,1,0:T(8,128)(2,1)} %copy-done.11), channel_id=1, source_target_pairs={{0,32},{32,0},{1,33},{33,1},{2,34},{34,2},{3,35},{35,3},{4,36},{36... | collective-permute-start | bytes 1572872 | tf_op jit(solution)/shard_map/ppermute | solution.py:100
  120.7 3.8 %collective-permute-start.18 = (bf16[4,64,1024]{2,1,0:T(8,128)(2,1)S(1)}, bf16[4,64,1024]{2,1,0:T(8,128)(2,1)S(1)}, u32[]{:S(2)}, u32[]{:S(2)}) collective-permute-start(bf16[4,64,1024]{2,1,0:T(8,128)(2,1)S(1)} %collective-permute-done.14.refs_8_), channel_id=1, source_target_pairs={{0,32},{32,0},{1,33},{33,1},{2,34},{34,2},{3,35},{35,3},{4,36},{36... | collective-permute-start | bytes 1572872 | tf_op jit(solution)/shard_map/ppermute | solution.py:100
  140.9 5.7 %collective-permute-start.19 = (bf16[32,2048]{1,0:T(8,128)(2,1)S(1)}, bf16[32,2048]{1,0:T(8,128)(2,1)S(1)}, u32[]{:S(2)}, u32[]{:S(2)}) collective-permute-start(bf16[32,2048]{1,0:T(8,128)(2,1)S(1)} %get-tuple-element.77), channel_id=1, source_target_pairs={{0,128},{1,129},{2,130},{3,131},{4,132},{5,133},{6,134},{7,135},{8... | collective-permute-start | bytes 393224 | tf_op jit(solution)/shard_map/ppermute | solution.py:320
  152.2 0.7 collective-permute-start.20
  158.3 0.7 collective-permute-start.21
  172.2 12.0 %collective-permute-start.22 = (bf16[32,2048]{1,0:T(8,128)(2,1)S(1)}, bf16[32,2048]{1,0:T(8,128)(2,1)S(1)}, u32[]{:S(2)}, u32[]{:S(2)}) collective-permute-start(bf16[32,2048]{1,0:T(8,128)(2,1)S(1)} %get-tuple-element.87), channel_id=1, source_target_pairs={{384,256},{385,257},{386,258},{387,259},{388,260},{389,261},{390,2... | collective-permute-start | bytes 393224 | tf_op jit(solution)/shard_map/ppermute | solution.py:333
  198.5 0.8 collective-permute-start.23
  207.1 18.6 %collective-permute-start.24 = (bf16[32,2048]{1,0:T(8,128)(2,1)S(1)}, bf16[32,2048]{1,0:T(8,128)(2,1)S(1)}, u32[]{:S(2)}, u32[]{:S(2)}) collective-permute-start(bf16[32,2048]{1,0:T(8,128)(2,1)S(1)} %get-tuple-element.91), channel_id=1, source_target_pairs={{128,0},{129,1},{130,2},{131,3},{132,4},{133,5},{134,6},{135,7},{1... | collective-permute-start | bytes 393224 | tf_op jit(solution)/shard_map/ppermute | solution.py:333
  259.1 64.8 %copy-start.17 = (f32[1,64,1024]{2,1,0:T(8,128)S(1)}, f32[1,64,1024]{2,1,0:T(8,128)}, u32[]{:S(2)}) copy-start(f32[1,64,1024]{2,1,0:T(8,128)} %param.15) | copy-start | bytes 786436
  259.1 64.8 %copy-start.19 = (f32[1,64,1024]{2,1,0:T(8,128)S(1)}, f32[1,64,1024]{2,1,0:T(8,128)}, u32[]{:S(2)}) copy-start(f32[1,64,1024]{2,1,0:T(8,128)} %param.20) | copy-start | bytes 786436
  259.1 64.8 %copy-start.20 = (f32[1,64,1024]{2,1,0:T(8,128)S(1)}, f32[1,64,1024]{2,1,0:T(8,128)}, u32[]{:S(2)}) copy-start(f32[1,64,1024]{2,1,0:T(8,128)} %param.21) | copy-start | bytes 786436
  324.1 6.3 %collective-permute-start.25 = (bf16[64,1024]{1,0:T(8,128)(2,1)S(1)}, bf16[64,1024]{1,0:T(8,128)(2,1)S(1)}, u32[]{:S(2)}, u32[]{:S(2)}) collective-permute-start(bf16[64,1024]{1,0:T(8,128)(2,1)S(1)} %fusion.8), channel_id=1, source_target_pairs={{32,0},{64,32},{96,64},{128,96},{160,128},{192,160},{224,192},{256... | collective-permute-start | bytes 393224 | tf_op jit(solution)/shard_map/ppermute | solution.py:364
  (18 other events, 110.5 us)
Sparse Core Ops, SparseCore 0:
  42.7 57.2 all-gather.4
  185.2 73.9 all-gather.6
